TPU v7x, 256 devices: a whole 4x4x8 slice. The times are simulated.
256 devices in a mesh: train: 32 (over y_hi, z, core), cand: 8 (over x, y_lo).
Axes of the slice: x: 4, y: 4 (y_hi: 2, y_lo: 2; y = y_hi * 2 + y_lo), z: 8, core: 2. Of those that a mesh axis runs over, the one named last changes fastest.
Arguments:
- x_train: float32 [8, 16384], P(None, 'train'), may hold values from -4 to 4
- x_cand: float32 [8, 8192], P(None, 'cand'), may hold values from -4 to 4
- targets: float32 [16384], P(('train', 'cand')), may hold values from -6 to 6
- noise: float32 [16384, 64], P(('train', 'cand')), may hold values from -5 to 5
- omega: float32 [8, 4096], replicated, may hold values from -6 to 6
- phase: float32 [4096], replicated, may hold values from -3.140625 to 3.140625
- prior_weights: bfloat16 [4096, 64], P('cand'), may hold values from -6 to 6
Outputs:
- samples: float32 [8192, 64], P(('cand', 'train'))
- solution: float32 [16384, 64], P(('train', 'cand'))
All inputs are finite; a program needn't handle non-finite values.
Results may differ from a plain program's by a relative error of at most 0.0019.
The roundings to bfloat16 on the way count: a program that leaves them out, or rounds other values in their place, can miss the bound.
Values may be sent and summed in bfloat16 or wider, within the bound.
A program may use at most 64 MiB of HBM per device.

v0:
```python
import math

import jax
import jax.numpy as jnp
from jax import lax
from jax.sharding import PartitionSpec as P

ITERS = 2


noise_level = 0.5


def squares_of(points):
    return jnp.sum(points * points, axis=0)


def kernel_tile(row_points, row_norms, column_points, column_norms):
    inner = jnp.dot(row_points.T, column_points, precision=lax.Precision.HIGHEST)
    return jnp.exp(-0.5 * (row_norms[:, None] + column_norms[None, :] - 2.0 * inner)).astype(
        jnp.bfloat16
    )


def features(points, omega, phase):
    angles = jnp.dot(points.T, omega, precision=lax.Precision.HIGHEST) + phase[None, :]
    return (math.sqrt(2.0 / omega.shape[1]) * jnp.cos(angles)).astype(jnp.bfloat16)


def kernel_rows(points, every_point, every_norm, weights):
    count = points.shape[1]
    size = math.gcd(count, 1024)
    stacked = points.reshape(points.shape[0], count // size, size).transpose(1, 0, 2)

    def one_block(block_points):
        tile = kernel_tile(block_points, squares_of(block_points), every_point, every_norm)
        return jnp.dot(tile, weights, preferred_element_type=jnp.float32)

    return lax.map(one_block, stacked).reshape(count, weights.shape[1])


def body(x_train, x_cand, targets, noise, omega, phase, prior_weights):
    own_rows = noise.shape[0]
    cand_index = lax.axis_index("cand")
    train_index = lax.axis_index("train")
    own_points = lax.dynamic_slice_in_dim(x_train, cand_index * own_rows, own_rows, 1)
    full_weights = lax.all_gather(prior_weights, "cand", axis=0, tiled=True)
    prior_train = jnp.dot(
        features(own_points, omega, phase), full_weights, preferred_element_type=jnp.float32
    )
    rhs = targets[:, None] - prior_train - noise
    column_points = lax.all_gather(x_train, "train", axis=1, tiled=True)
    row_norms = squares_of(own_points)
    column_norms = squares_of(column_points)
    width = max(128, 262144 // own_points.shape[1])

    def squares(values):
        return lax.psum(jnp.sum(values * values, axis=0), ("train", "cand"))

    solution = jnp.zeros(rhs.shape, jnp.float32)
    residual = rhs
    direction = rhs
    norm_now = squares(residual)
    for step in range(ITERS):
        packed = direction.astype(jnp.bfloat16)
        empty = jnp.zeros((own_points.shape[1], packed.shape[1]), jnp.float32)
        total = empty
        piece = lax.all_gather(packed, ("train", "cand"), axis=0, tiled=True)
        for offset in range(0, piece.shape[0], width):
            count = min(width, piece.shape[0] - offset)
            accumulate_points = lax.dynamic_slice_in_dim(column_points, offset, count, 1)
            norms = lax.dynamic_slice_in_dim(column_norms, offset, count, 0)
            tile = kernel_tile(own_points, row_norms, accumulate_points, norms)
            total = total + jnp.dot(
                tile, piece[offset : offset + count], preferred_element_type=jnp.float32
            )
        image = total + noise_level * direction
        curve = lax.psum(jnp.sum(direction * image, axis=0), ("train", "cand"))
        alpha = norm_now / curve
        solution = solution + alpha * direction
        residual = residual - alpha * image
        norm_next = squares(residual)
        direction = residual + norm_next / norm_now * direction
        norm_now = norm_next
    per_device = x_cand.shape[1] // lax.axis_size("train")
    mine = lax.dynamic_slice_in_dim(x_cand, train_index * per_device, per_device, 1)
    packed_solution = solution.astype(jnp.bfloat16)
    block_weights = lax.all_gather(packed_solution, "cand", axis=0, tiled=True)
    train_norms = squares_of(x_train)
    kernel_part = lax.psum_scatter(
        kernel_rows(x_cand, x_train, train_norms, block_weights),
        "train",
        scatter_dimension=0,
        tiled=True,
    )
    prior_cand = jnp.dot(
        features(mine, omega, phase), full_weights, preferred_element_type=jnp.float32
    )
    return (prior_cand + kernel_part, solution)


def solution(mesh):
    placed = (
        P(None, "train"),
        P(None, "cand"),
        P(("train", "cand")),
        P(("train", "cand"), None),
        P(),
        P(),
        P("cand", None),
    )
    return jax.shard_map(
        body,
        mesh=mesh,
        in_specs=placed,
        out_specs=(P(("cand", "train"), None), P(("train", "cand"), None)),
        check_vma=False,
    )
```

profile of v0, /device:TPU:1, one launch (start us, length us, event | category | flops | bytes accessed | tf_op | source)
XLA Modules:
  0.0 1844.4 jit_solution(14359610649674526647)
XLA Ops:
  7.2 24.8 %all_gather.15 = bf16[4096,64]{0,1:T(8,128)(2,1)S(1)} all-gather(bf16[512,64]{0,1:T(8,128)(2,1)} %param.13), channel_id=1, replica_groups=mesh['train'=32,'cand'=8] {'cand'}, dimensions={0}, use_global_device_ids=true | all-gather | bytes 589824 | tf_op jit(solution)/shard_map/all_gather | solution.py:47
  32.1 5.5 fusion.14
  37.5 1.7 fusion.56
  40.1 52.3 %all_gather.16 = f32[8,16384]{1,0:T(8,128)S(1)} all-gather(f32[8,512]{1,0:T(8,128)} %param.7), channel_id=1, replica_groups=mesh['train'=32,'cand'=8] {'train'}, dimensions={1}, use_global_device_ids=true | all-gather | bytes 540672 | tf_op jit(solution)/shard_map/all_gather | solution.py:52
  92.6 1.9 fusion.15
  97.1 1.2 fusion.18
  98.3 656.3 %all-gather.3.cloned.1.call-done = bf16[16384,64]{1,0:T(8,128)(2,1)} async-done(((bf16[64,64]{1,0:T(8,128)(2,1)}), bf16[16384,64]{1,0:T(8,128)(2,1)}) %all-gather.3.cloned.1.call-update) | async-done | bytes 2097168 | tf_op jit(solution)/shard_map/all_gather | solution.py:68
  754.6 1.5 fusion.35
  756.2 1.5 convolution_add_fusion.7
  757.7 1.5 convolution_add_fusion.6
  759.3 1.6 multiply_reduce_fusion.2
  760.8 78.7 %all-reduce = (f32[64]{0:T(128)S(1)}, f32[64]{0:T(128)S(1)}) all-reduce(f32[64]{0:T(128)S(1)} %get-tuple-element.15, f32[64]{0:T(128)S(1)} %get-tuple-element.14), channel_id=1, replica_groups=mesh['train'=32,'cand'=8] {'train','cand'}, use_global_device_ids=true, to_apply=%region_3.0 | all-reduce | flops 128 | bytes 1024 | tf_op jit(solution)/shard_map/psum | solution.py:58
  839.6 72.7 %psum.30 = f32[64]{0:T(128)S(1)} all-reduce(f32[64]{0:T(128)S(1)} %multiply_reduce_fusion.1), channel_id=1, replica_groups=mesh['train'=32,'cand'=8] {'train','cand'}, use_global_device_ids=true, to_apply=%region_9.0 | all-reduce | flops 64 | bytes 512 | tf_op jit(solution)/shard_map/psum | solution.py:58
  913.2 2.2 exponential_convert_fusion
  915.4 702.0 %all-gather.5.cloned.1.call-done = bf16[16384,64]{1,0:T(8,128)(2,1)} async-done(((bf16[64,64]{1,0:T(8,128)(2,1)}), bf16[16384,64]{1,0:T(8,128)(2,1)}) %all-gather.5.cloned.1.call-update) | async-done | bytes 2097168 | tf_op jit(solution)/shard_map/all_gather | solution.py:68
  1617.4 1.7 fusion.30
  1619.1 1.5 convolution_add_fusion.4
  1620.6 1.5 convolution_add_fusion.3
  1622.2 1.6 fusion.26
  1623.7 78.5 %psum.31 = f32[64]{0:T(128)S(1)} all-reduce(f32[64]{0:T(128)S(1)} %fusion.26), channel_id=1, replica_groups=mesh['train'=32,'cand'=8] {'train','cand'}, use_global_device_ids=true, to_apply=%region_11.12 | all-reduce | flops 64 | bytes 512 | tf_op jit(solution)/shard_map/psum | solution.py:78
  1702.9 21.9 %all_gather.19 = bf16[512,64]{1,0:T(8,128)(2,1)S(1)} all-gather(bf16[64,64]{1,0:T(8,128)(2,1)S(1)} %get-tuple-element.24), channel_id=1, replica_groups=mesh['train'=32,'cand'=8] {'cand'}, dimensions={0}, use_global_device_ids=true | all-gather | bytes 73728 | tf_op jit(solution)/shard_map/all_gather | solution.py:88
  1726.1 2.7 fusion.21
  1728.8 107.5 %reduce-scatter.2.cloned.1.call-done = f32[32,64]{1,0:T(8,128)} async-done(((f32[1024,64]{1,0:T(8,128)}), f32[32,64]{1,0:T(8,128)}) %reduce-scatter.2.cloned.1.call-update) | async-done | bytes 8208 | tf_op jit(solution)/shard_map/reduce_scatter | solution.py:90
  1836.3 1.6 convolution_add_fusion.8
  (30 shorter events, 6.4 us)
Async XLA Ops:
  7.2 24.9 %copy-start = (f32[8,4096]{1,0:T(8,128)S(1)}, f32[8,4096]{1,0:T(8,128)}, u32[]{:S(2)}) copy-start(f32[8,4096]{1,0:T(8,128)} %param.11) | copy-start | bytes 393220
  7.2 87.3 %copy-start.1 = (f32[8,512]{1,0:T(8,128)S(1)}, f32[8,512]{1,0:T(8,128)}, u32[]{:S(2)}) copy-start(f32[8,512]{1,0:T(8,128)} %param.7) | copy-start | bytes 49156
  7.2 747.4 %all-gather.3.cloned.1.call-start = ((), (), s32[]{:S(2)}) async-start(), calls=%async_computation.1 | async-start | bytes 4210688 | tf_op jit(solution)/shard_map/all_gather | solution.py:68
  39.3 1578.1 %all-gather.5.cloned.1.call-start = ((), (), s32[]{:S(2)}) async-start(), calls=%async_computation.2 | async-start | bytes 4210688 | tf_op jit(solution)/shard_map/all_gather | solution.py:68
  97.0 816.1 %copy-start.3 = (f32[8,1024]{1,0:T(8,128)S(1)}, f32[8,1024]{1,0:T(8,128)}, u32[]{:S(2)}) copy-start(f32[8,1024]{1,0:T(8,128)} %param.8) | copy-start | bytes 98308
  98.3 661.0 %copy-start.4 = (bf16[64,4096]{1,0:T(8,128)(2,1)}, bf16[64,4096]{1,0:T(8,128)(2,1)S(1)}, u32[]{:S(2)}) copy-start(bf16[64,4096]{1,0:T(8,128)(2,1)S(1)} %fusion.18) | copy-start | bytes 1572868
  912.9 923.3 %reduce-scatter.2.cloned.1.call-start = ((), (), s32[]{:S(2)}) async-start(), calls=%async_computation.3 | async-start | bytes 540672 | tf_op jit(solution)/shard_map/reduce_scatter | solution.py:90
  915.4 810.7 %copy-start.2 = (f32[4096]{0:T(1024)S(1)}, f32[4096]{0:T(1024)}, u32[]{:S(2)}) copy-start(f32[4096]{0:T(1024)} %param.12) | copy-start | bytes 49156
Sparse Core Ops, SparseCore 0:
  39.4 715.1 all-gather.2
  913.0 704.2 all-gather.4
  1726.2 110.0 reduce-scatter.1
where the time goes:
time: 1850 us; the launch traced here: 1840 us
  waiting for transfers between devices  1470 us (79%)
  blocking collectives  329 us (18%)
  matrix products  33.1 us (2%)
    all_gather x2, waiting for transfers between devices, body(): piece = lax.all_gather(packed, ('train', 'cand'), axis=0, tiled=True)  1360 us
    psum x2, blocking collectives, squares(): return lax.psum(jnp.sum(values * values, axis=0), ('train', 'cand'))  151 us
    reduce_scatter x1, waiting for transfers between devices, body(): lax.psum_scatter(kernel_rows(x_cand, x_train, train_norms, block_weights)...  107 us
    psum x1, blocking collectives, body(): curve = lax.psum(jnp.sum(direction * image, axis=0), ('train', 'cand'))  78.5 us
    all_gather x1, blocking collectives, body(): column_points = lax.all_gather(x_train, 'train', axis=1, tiled=True)  52.3 us
  transfers between devices with their start and end apart: 3, of which 3 were waited for; matrix products, arithmetic and copies ran while one was open for 1% of the time, Pallas kernels for 0%

commit v1 on v0

v1 whole, which is shorter than its diff:
```python
import math

import jax
import jax.numpy as jnp
from jax import lax
from jax.experimental import pallas as pl
from jax.experimental.pallas import tpu as pltpu
from jax.sharding import PartitionSpec as P

MESH = pl.DeviceIdType.MESH
F32, BF16 = jnp.float32, jnp.bfloat16
NZ, NC, NH = 8, 8, 4
NP = NH * NC
OWN = 64
CANDS = 32
FEATS = 512
TOTAL_FEATS = 4096
NOISE_LEVEL = 0.5
COS = (
    0.9999999890590217,
    -19.73920449945381,
    64.93911745989173,
    -85.45013953082398,
    60.16763095051855,
    -25.967599246994247,
    6.528658159389057,
)


def split3(value):
    one = value.astype(BF16).astype(F32)
    two = (value - one).astype(BF16).astype(F32)
    return one, two, value - one - two


def rows8(*rows):
    index = lax.broadcasted_iota(jnp.int32, (8, rows[0].shape[1]), 0)
    out = jnp.zeros((8, rows[0].shape[1]), F32)
    for place, row in enumerate(rows):
        out = jnp.where(index == place, row, out)
    return out


def half_norm(points):
    return -0.5 * jnp.sum(points * points, axis=0, keepdims=True)


def left_side(points):
    one, two, three = split3(points)
    ones = jnp.ones((1, points.shape[1]), F32)
    tail = rows8(*split3(half_norm(points)), ones, ones, ones)
    pad = jnp.zeros((72, points.shape[1]), F32)
    return jnp.concatenate([one, one, two, two, one, three, tail, pad], axis=0).T.astype(BF16)


def right_side(points, tail):
    one, two, three = split3(points)
    pad = jnp.zeros((72, points.shape[1]), F32)
    return jnp.concatenate([one, two, one, two, three, one, tail, pad], axis=0).astype(BF16)


def kernel(
    xt, xc, tg, nz, om, ph, pw, sam, sol,
    xls, xl, xcs, xcb, xp, by, bw, atb, atc, atl, km, pwd,
    pts, ptb, pcs, pcb, own0, own1, vb0, vb1, r0l, r1l,
    o1, o2, kr, krb, kr1, ucs, ucb, vcs, vcb,
    sa_s, sa, sb_s, sb, ra_s, ra, rb_s, rb, qa_s, qa, qb_s, qb,
    hb0, hb1, ssem, rsem,
):
    t, c = lax.axis_index("train"), lax.axis_index("cand")
    y_hi, z, core = t // 16, lax.rem(t, 16) // 2, lax.rem(t, 2)
    h = y_hi * 2 + core
    q = h * NC + c

    def plane_peer(k):
        other = lax.rem(q + k, NP)
        oh, oc = other // NC, lax.rem(other, NC)
        return ((oh // 2) * 16 + z * 2 + lax.rem(oh, 2), oc)

    def line_index(k):
        return lax.rem(z + k, NZ)

    def line_peer(k):
        return (y_hi * 16 + line_index(k) * 2 + core, c)

    def cand_index(k):
        return lax.rem(c + k, NC)

    def cand_peer(k):
        return (t, cand_index(k))

    def block_peer(k):
        oh = lax.rem(h + k, NH)
        return ((oh // 2) * 16 + z * 2 + lax.rem(oh, 2), c)

    barrier = pltpu.get_barrier_semaphore()

    def greet(peer, count):
        def one(k, carry):
            pl.semaphore_signal(barrier, inc=1, device_id=peer(k), device_id_type=MESH)
            return carry

        lax.fori_loop(1, count, one, 0)

    greet(plane_peer, NP)
    greet(line_peer, NZ)

    def push(phase, count, peer, source, target):
        def one(k, carry):
            pltpu.make_async_remote_copy(
                src_ref=source(k),
                dst_ref=target,
                send_sem=ssem.at[phase],
                recv_sem=rsem.at[phase],
                device_id=peer(k),
                device_id_type=MESH,
            ).start()
            return carry

        lax.fori_loop(1, count, one, 0)

    def settle(phase, sems, buf):
        ref = buf.at[pl.ds(0, buf.shape[0] - 1)]
        pltpu.make_async_copy(ref, ref, sems.at[phase]).wait()

    def arrived(phase, buf):
        settle(phase, rsem, buf)

    lane = lax.broadcasted_iota(jnp.int32, (1, 128), 1)
    low = lane < 64

    def swap(value):
        return pltpu.roll(value, 64, 1)

    def pair(first, second):
        return jnp.where(low, first, swap(second))

    def fold(value):
        row = jnp.sum(value, axis=0, keepdims=True)
        return row + swap(row)

    mine = xt[:, pl.ds(pl.multiple_of((c // 2) * 128, 128), 128)]
    mine = jnp.where(lax.rem(c, 2) == 1, swap(mine), mine)
    xls[...] = mine
    xl[z] = mine
    xp[h] = xt[...]
    cand = xc[:, pl.ds(pl.multiple_of((t // 4) * 128, 128), 128)]
    cand = pltpu.roll(cand, lax.rem(128 - lax.rem(t, 4) * 32, 128), 1)
    xcs[...] = cand
    xcb[c] = cand

    feat = pl.ds(pl.multiple_of(c * FEATS, FEATS), FEATS)
    turn = 1.0 / (2.0 * math.pi)
    zero = jnp.zeros((1, FEATS), F32)
    bw[...] = right_side(
        om[:, feat] * turn, rows8(zero, zero, zero, *split3(ph[:, feat] * turn))
    )
    pwd[...] = jnp.concatenate([pw[...], pw[...]], axis=1)
    atb[...] = left_side(xt[...])

    def feature_rows(left, first, count):
        turns = jnp.dot(left[pl.ds(first, count), :], bw[...], preferred_element_type=F32)
        part = turns - jnp.floor(turns + 0.5)
        square = part * part
        value = jnp.full(square.shape, COS[-1], F32)
        for coefficient in COS[-2::-1]:
            value = value * square + coefficient
        packed = (value * math.sqrt(2.0 / TOTAL_FEATS)).astype(BF16)
        return jnp.dot(packed, pwd[...], preferred_element_type=F32)

    def train_features(i, carry):
        out = feature_rows(atb, pl.multiple_of(i * OWN, OWN), OWN)
        pts[i] = jnp.where(low, out[0:32], out[32:64])
        return carry

    lax.fori_loop(0, NC, train_features, 0)

    pl.semaphore_wait(barrier, NP - 1 + NZ - 1)
    push(0, NH, block_peer, lambda k: xt, xp.at[h])
    push(1, NZ, line_peer, lambda k: xls, xl.at[z])
    push(3, NC, cand_peer, lambda k: pts.at[cand_index(k)], ptb.at[c])
    push(2, NC, cand_peer, lambda k: xcs, xcb.at[c])
    ptb[c] = pts[c]

    row = tg[...]
    place = lax.broadcasted_iota(jnp.int32, (32, 64), 0)
    at = lax.broadcasted_iota(jnp.int32, (32, 64), 1)
    upper = jnp.sum(jnp.where(at == place, row, 0.0), axis=1, keepdims=True)
    lower = jnp.sum(jnp.where(at == place + 32, row, 0.0), axis=1, keepdims=True)
    noise = jnp.concatenate([nz[0:32, :], nz[32:64, :]], axis=1)
    base = jnp.where(low, upper, lower) - noise

    def line_cands(j):
        tile = xc[:, pl.ds(pl.multiple_of(y_hi * 512 + j * 128, 128), 128)]
        tile = pltpu.roll(tile, lax.rem(128 - core * 32, 128), 1)
        return jnp.where(lane < 32, tile, pltpu.roll(tile, 96, 1))

    for j in range(2):
        atl[512 + j * 128 : 640 + j * 128, :] = left_side(
            pair(line_cands(2 * j), line_cands(2 * j + 1))
        )

    arrived(0, xp)
    for i in range(NH):
        uppers, lowers = [], []
        for j in range(2):
            tiles = [xp[i, :, j * 256 + 128 * g : j * 256 + 128 * g + 128] for g in range(2)]
            uppers.append(pair(*[jnp.where(lane < 32, a, pltpu.roll(a, 96, 1)) for a in tiles]))
            lowers.append(
                pair(*[jnp.where(lane < 32, pltpu.roll(a, 96, 1), swap(a)) for a in tiles])
            )
        for start, tiles in ((i * 256, uppers), (1024 + i * 256, lowers)):
            points = jnp.concatenate(tiles, axis=1)
            ones = jnp.ones((1, 256), F32)
            tail = rows8(ones, ones, ones, *split3(half_norm(points)))
            by[:, start : start + 256] = right_side(points, tail)

    def entries(first, count):
        def one(j, carry):
            columns = pl.ds(pl.multiple_of(j * 256, 256), 256)
            power = jnp.dot(atl[pl.ds(first, count), :], by[:, columns], preferred_element_type=F32)
            km[pl.ds(first, count), columns] = jnp.exp(power).astype(BF16)
            return carry

        lax.fori_loop(0, 8, one, 0)

    arrived(1, xl)
    for j in range(4):
        atl[j * 128 : j * 128 + 128, :] = left_side(pair(xl[2 * j], xl[2 * j + 1]))
    entries(0, 256)

    arrived(3, ptb)
    r0 = base - jnp.sum(ptb[...], axis=0)
    own0[...] = r0
    r0l[z] = r0
    hb0[...] = r0.astype(BF16)
    vb0[q] = r0.astype(BF16)
    push(4, NP, plane_peer, lambda k: hb0, vb0.at[q])
    push(5, NZ, line_peer, lambda k: own0, r0l.at[z])
    rr_own = fold(r0 * r0)

    entries(256, 256)
    entries(512, 256)

    arrived(2, xcb)
    for j in range(2):
        joined = xcb[4 * j]
        for g in range(1, 4):
            joined = jnp.where(lane < 32 * g, joined, pltpu.roll(xcb[4 * j + g], 32 * g, 1))
        atc[j * 128 : j * 128 + 128, :] = left_side(joined)

    def cand_features(i, carry):
        out = feature_rows(atc, pl.multiple_of(i * OWN, OWN), OWN)
        pcs[2 * i] = jnp.where(low, out[0:16], out[16:32])
        pcs[2 * i + 1] = jnp.where(low, out[32:48], out[48:64])
        return carry

    lax.fori_loop(0, 4, cand_features, 0)
    push(6, NC, cand_peer, lambda k: pcs.at[cand_index(k)], pcb.at[c])
    pcb[c] = pcs[c]

    def product(field, pieces, cand_pieces):
        values = field[...].reshape(NP * 32, 128)
        o1[...] = jnp.dot(km[:, 0:1024], values, preferred_element_type=F32)
        o2[...] = jnp.dot(km[:, 1024:2048], values, preferred_element_type=F32)

        def joined(first, size):
            a1, b1 = o1[pl.ds(first, size), :], o1[pl.ds(first + size, size), :]
            a2, b2 = o2[pl.ds(first, size), :], o2[pl.ds(first + size, size), :]
            return jnp.where(low, a1, b2) + swap(jnp.where(low, b1, a2))

        for i in range(NZ):
            pieces[i] = joined(i * 64, 32)
        for i in range(NZ):
            cand_pieces[i] = joined(512 + i * 32, 16)

    arrived(4, vb0)
    product(vb0, kr, ucs)
    push(7, NZ, line_peer, lambda k: kr.at[line_index(k)], krb.at[z])
    krb[z] = kr[z]
    arrived(5, r0l)
    curve = fold(jnp.sum(kr[...] * r0l[...], axis=0))
    part = jnp.where(low, curve, rr_own)
    sa_s[...] = part
    sa[q] = part
    push(8, NP, plane_peer, lambda k: sa_s, sa.at[q])
    push(9, NZ, line_peer, lambda k: ucs.at[line_index(k)], ucb.at[z])
    ucb[z] = ucs[z]
    arrived(8, sa)
    part = jnp.sum(sa[...], axis=0)
    sb_s[...] = part
    sb[z] = part
    push(10, NZ, line_peer, lambda k: sb_s, sb.at[z])
    arrived(7, krb)
    r0 = own0[...]
    image = jnp.sum(krb[...], axis=0) + NOISE_LEVEL * r0
    arrived(10, sb)
    part = jnp.sum(sb[...], axis=0)
    other = swap(part)
    rr0 = jnp.where(low, other, part)
    alpha1 = rr0 / (jnp.where(low, part, other) + NOISE_LEVEL * rr0)
    r1 = r0 - alpha1 * image

    own1[...] = r1
    r1l[z] = r1
    hb1[...] = r1.astype(BF16)
    vb1[q] = r1.astype(BF16)
    push(11, NP, plane_peer, lambda k: hb1, vb1.at[q])
    rr1_own = fold(r1 * r1)
    ra_s[...] = rr1_own
    ra[q] = rr1_own
    push(13, NP, plane_peer, lambda k: ra_s, ra.at[q])
    push(12, NZ, line_peer, lambda k: own1, r1l.at[z])
    arrived(13, ra)
    part = jnp.sum(ra[...], axis=0)
    rb_s[...] = part
    rb[z] = part
    push(14, NZ, line_peer, lambda k: rb_s, rb.at[z])
    arrived(11, vb1)
    product(vb1, kr1, vcs)
    push(15, NZ, line_peer, lambda k: vcs.at[line_index(k)], vcb.at[z])
    vcb[z] = vcs[z]
    arrived(12, r1l)
    arrived(14, rb)
    rr1 = jnp.sum(rb[...], axis=0)
    beta = rr1 / rr0
    curve = fold(jnp.sum((r1l[...] + beta * r0l[...]) * (kr1[...] + beta * kr[...]), axis=0))
    r0, r1 = own0[...], own1[...]
    d1 = r1 + beta * r0
    part = curve + NOISE_LEVEL * fold(d1 * d1)
    qa_s[...] = part
    qa[q] = part
    push(16, NP, plane_peer, lambda k: qa_s, qa.at[q])
    arrived(6, pcb)
    prior = jnp.sum(pcb[...], axis=0)
    arrived(9, ucb)
    first_part = jnp.sum(ucb[...], axis=0)
    arrived(16, qa)
    part = jnp.sum(qa[...], axis=0)
    qb_s[...] = part
    qb[z] = part
    push(17, NZ, line_peer, lambda k: qb_s, qb.at[z])
    arrived(15, vcb)
    second_part = jnp.sum(vcb[...], axis=0)
    arrived(17, qb)
    alpha2 = rr1 / jnp.sum(qb[...], axis=0)

    result = alpha1 * r0 + alpha2 * d1
    sol[0:32, :] = result[:, 0:64]
    sol[32:64, :] = swap(result)[:, 0:64]
    result = prior + (alpha1 + alpha2 * beta) * first_part + alpha2 * second_part
    sam[0:16, :] = result[:, 0:64]
    sam[16:32, :] = swap(result)[:, 0:64]

    for phase, buf in enumerate(
        (xp, xl, xcb, ptb, vb0, r0l, pcb, krb, sa, ucb, sb, vb1, r1l, ra, rb, vcb, qa, qb)
    ):
        settle(phase, ssem, buf)


def body(x_train, x_cand, targets, noise, omega, phase, prior_weights):
    vmem = pltpu.VMEM
    field = lambda n, rows, dtype=F32: vmem((n, rows, 128), dtype)
    tile, row = vmem((8, 128), F32), vmem((1, 128), F32)
    scratch = [
        tile, field(NZ, 8), tile, field(NC, 8), vmem((NH, 8, 512), F32),
        vmem((128, 2048), BF16), vmem((128, FEATS), BF16), vmem((512, 128), BF16),
        vmem((256, 128), BF16), vmem((768, 128), BF16), vmem((768, 2048), BF16),
        vmem((FEATS, 128), BF16),
        field(NC, 32), field(NC, 32), field(NC, 16), field(NC, 16),
        vmem((32, 128), F32), vmem((32, 128), F32),
        field(NP, 32, BF16), field(NP, 32, BF16), field(NZ, 32), field(NZ, 32),
        vmem((768, 128), F32), vmem((768, 128), F32),
        field(NZ, 32), field(NZ, 32), field(NZ, 32),
        field(NZ, 16), field(NZ, 16), field(NZ, 16), field(NZ, 16),
        row, field(NP, 1), row, field(NZ, 1), row, field(NP, 1), row, field(NZ, 1),
        row, field(NP, 1), row, field(NZ, 1),
        vmem((32, 128), BF16), vmem((32, 128), BF16),
        pltpu.SemaphoreType.DMA((18,)), pltpu.SemaphoreType.DMA((18,)),
    ]
    return pl.pallas_call(
        kernel,
        out_shape=(
            jax.ShapeDtypeStruct((CANDS, OWN), F32),
            jax.ShapeDtypeStruct((OWN, OWN), F32),
        ),
        in_specs=[pl.BlockSpec(memory_space=vmem)] * 7,
        out_specs=(pl.BlockSpec(memory_space=vmem),) * 2,
        scratch_shapes=scratch,
        compiler_params=pltpu.CompilerParams(
            collective_id=0, has_side_effects=True, vmem_limit_bytes=32 * 1024 * 1024
        ),
    )(
        x_train, x_cand, targets.reshape(1, OWN), noise, omega,
        phase.reshape(1, TOTAL_FEATS), prior_weights,
    )


def solution(mesh):
    placed = (
        P(None, "train"),
        P(None, "cand"),
        P(("train", "cand")),
        P(("train", "cand"), None),
        P(),
        P(),
        P("cand", None),
    )
    return jax.shard_map(
        body,
        mesh=mesh,
        in_specs=placed,
        out_specs=(P(("cand", "train"), None), P(("train", "cand"), None)),
        check_vma=False,
    )
```

time: 1850 us -> 58.7 us (0.03)
  waiting for transfers between devices: 1470 us -> 0 us
  blocking collectives: 329 us -> 0 us
  Pallas kernels: 0 us -> 54 us
  matrix products: 33.1 us -> 0 us
    all_gather x2 -> x0, waiting for transfers between devices: 1360 us -> none  [body(): piece = lax.all_gather(packed, ('train', 'cand'), axis=0, tiled=True)]
    psum x3 -> x0, blocking collectives: 230 us -> none  [the longest x2 151 us: squares(): return lax.psum(jnp.sum(values * values, axis=0), ('train', 'cand'))]
    reduce_scatter x1 -> x0, waiting for transfers between devices: 107 us -> none  [body(): lax.psum_scatter(kernel_rows(x_cand, x_train, train_norms, block_weights)...]
    all_gather x3 -> x0, blocking collectives: 99 us -> none  [the longest x1 52.3 us: body(): column_points = lax.all_gather(x_train, 'train', axis=1, tiled=True)]
    pallas_call x0 -> x1, Pallas kernels: none -> 54 us  [body(): pl.pallas_call(kernel, out_shape=(jax.ShapeDtypeStruct((CANDS, OWN), F32)...]
    dot_general x18 -> x0, matrix products: 33.1 us -> none  [the longest x8 12.5 us: body(): jnp.dot(tile, piece[offset:offset + count], preferred_element_type=jnp.fl...]
  transfers between devices with their start and end apart: 3 -> 0, of which waited for: 3 -> 0; matrix products, arithmetic and copies ran while one was open for 1% -> 0% of each run, Pallas kernels for 0% -> 0%
where the time goes in v1:
time: 58.7 us; the launch traced here: 58.4 us
  Pallas kernels  54 us (92%)
  local copies, waits for them, and re-layouts  3.69 us (6%)
  between operations  0.72 us (1%)
    pallas_call x1, Pallas kernels, body(): pl.pallas_call(kernel, out_shape=(jax.ShapeDtypeStruct((CANDS, OWN), F32)...  54 us
    unnamed x15, local copies, waits for them, and re-layouts  3.69 us

profile of v1, /device:TPU:1, one launch (start us, length us, event | category | flops | bytes accessed | tf_op | source)
XLA Modules:
  0.0 58.4 jit_solution(8763134348543346164)
XLA Ops:
  0.6 0.0 copy-start
  0.6 0.0 copy-start.1
  0.7 0.0 copy-start.2
  0.7 0.0 copy-start.5
  0.7 1.0 %copy.9.pw = bf16[512,64]{1,0:T(8,128)(2,1)S(1)} copy(bf16[512,64]{0,1:T(8,128)(2,1)} %param.13) | data formatting | bytes 131072 | tf_op args[6]
  1.7 0.0 copy-done
  1.7 0.0 copy-done.1
  1.7 0.0 copy-done.2
  1.7 0.0 copy-done.5
  1.7 0.0 copy-start.3
  1.8 0.7 %copy-done.3 = f32[8,512]{1,0:T(8,128)S(1)} copy-done((f32[8,512]{1,0:T(8,128)S(1)}, f32[8,512]{1,0:T(8,128)}, u32[]{:S(2)}) %copy-start.3) | copy-done | bytes 16408
  2.5 0.0 copy-start.4
  2.5 0.7 %copy-done.4 = f32[4096]{0:T(1024)S(1)} copy-done((f32[4096]{0:T(1024)S(1)}, f32[4096]{0:T(1024)}, u32[]{:S(2)}) %copy-start.4) | copy-done | bytes 16408
  3.2 54.0 %shard_map.86 = (f32[32,64]{1,0:T(8,128)S(1)}, f32[64,64]{1,0:T(8,128)S(1)}) custom-call(f32[8,512]{1,0:T(8,128)S(1)} %copy-done.3, f32[8,1024]{1,0:T(8,128)S(1)} %copy-done.1, f32[1,64]{1,0:T(1,128)S(1)} %bitcast.3, f32[64,64]{1,0:T(8,128)S(1)} %copy-done.2, f32[8,4096]{1,0:T(8,128)S(1)} %copy-done, f32[1,4096]{1,0:T(1,128)S(1)} %bitcast.2, ...), custom_call_target="tpu_custom_call" | custom-call | tf_op jit(solution)/shard_map/pallas_call | solution.py:381
  57.2 0.6 %copy.12 = f32[32,64]{1,0:T(8,128)} copy(f32[32,64]{1,0:T(8,128)S(1)} %get-tuple-element.4) | data formatting | bytes 16384
  57.8 0.6 %copy.13 = f32[64,64]{1,0:T(8,128)} copy(f32[64,64]{1,0:T(8,128)S(1)} %get-tuple-element.5) | data formatting | bytes 32768
Async XLA Ops:
  0.6 1.1 %copy-start = (f32[8,4096]{1,0:T(8,128)S(1)}, f32[8,4096]{1,0:T(8,128)}, u32[]{:S(2)}) copy-start(f32[8,4096]{1,0:T(8,128)} %om.1) | copy-start | bytes 393220
  0.6 1.1 %copy-start.1 = (f32[8,1024]{1,0:T(8,128)S(1)}, f32[8,1024]{1,0:T(8,128)}, u32[]{:S(2)}) copy-start(f32[8,1024]{1,0:T(8,128)} %xc.1) | copy-start | bytes 98308
  0.7 1.1 %copy-start.2 = (f32[64,64]{1,0:T(8,128)S(1)}, f32[64,64]{1,0:T(8,128)}, u32[]{:S(2)}) copy-start(f32[64,64]{1,0:T(8,128)} %nz.1) | copy-start | bytes 49156
  0.7 1.1 %copy-start.5 = (f32[64]{0:T(128)S(1)}, f32[64]{0:T(128)}, u32[]{:S(2)}) copy-start(f32[64]{0:T(128)} %param.9) | copy-start | bytes 772
  1.7 0.7 %copy-start.3 = (f32[8,512]{1,0:T(8,128)S(1)}, f32[8,512]{1,0:T(8,128)}, u32[]{:S(2)}) copy-start(f32[8,512]{1,0:T(8,128)} %xt.1) | copy-start | bytes 49156
  2.5 0.7 %copy-start.4 = (f32[4096]{0:T(1024)S(1)}, f32[4096]{0:T(1024)}, u32[]{:S(2)}) copy-start(f32[4096]{0:T(1024)} %param.12) | copy-start | bytes 49156

commit v2 on v1

--- a/solution.py
+++ b/solution.py
@@ -60,12 +60,13 @@
 
 
 def kernel(
-    xt, xc, tg, nz, om, ph, pw, sam, sol,
-    xls, xl, xcs, xcb, xp, by, bw, atb, atc, atl, km, pwd,
-    pts, ptb, pcs, pcb, own0, own1, vb0, vb1, r0l, r1l,
-    o1, o2, kr, krb, kr1, ucs, ucb, vcs, vcb,
+    xt_hbm, xc_hbm, tg_hbm, nz_hbm, om_hbm, ph_hbm, pw_hbm, sam, sol,
+    xt, xc, tg, nz, om, ph, pw,
+    xls, xl, xcs, xcb, xp, by, bw, atl, km,
+    pts, ptb, pcs, pcb, own0, own1, vb0, vb1, r0l, q0l,
+    o1, o2, kr, krb, kq, ucs, ucb, wcs, wcb,
     sa_s, sa, sb_s, sb, ra_s, ra, rb_s, rb, qa_s, qa, qb_s, qb,
-    hb0, hb1, ssem, rsem,
+    hb0, hb1, isem, ssem, rsem,
 ):
     t, c = lax.axis_index("train"), lax.axis_index("cand")
     y_hi, z, core = t // 16, lax.rem(t, 16) // 2, lax.rem(t, 2)
@@ -92,6 +93,25 @@
     def block_peer(k):
         oh = lax.rem(h + k, NH)
         return ((oh // 2) * 16 + z * 2 + lax.rem(oh, 2), c)
+
+    feat = pl.ds(pl.multiple_of(c * FEATS, FEATS), FEATS)
+    inputs = [
+        pltpu.make_async_copy(source, target, isem.at[number])
+        for number, (source, target) in enumerate(
+            (
+                (xt_hbm, xt),
+                (om_hbm.at[:, feat], om),
+                (ph_hbm.at[:, feat], ph),
+                (pw_hbm, pw.at[pl.ds(0, OWN)]),
+                (pw_hbm, pw.at[pl.ds(OWN, OWN)]),
+                (xc_hbm, xc),
+                (tg_hbm, tg),
+                (nz_hbm, nz),
+            )
+        )
+    ]
+    for copy in inputs:
+        copy.start()
 
     barrier = pltpu.get_barrier_semaphore()
 
@@ -139,6 +159,31 @@
         row = jnp.sum(value, axis=0, keepdims=True)
         return row + swap(row)
 
+    for copy in inputs[:5]:
+        copy.wait()
+
+    turn = 1.0 / (2.0 * math.pi)
+    zero = jnp.zeros((1, FEATS), F32)
+    bw[...] = right_side(om[...] * turn, rows8(zero, zero, zero, *split3(ph[...] * turn)))
+    def prior_share(left):
+        turns = jnp.dot(left, bw[...], preferred_element_type=F32)
+        part = turns - jnp.floor(turns + 0.5)
+        square = part * part
+        value = jnp.full(square.shape, COS[-1], F32)
+        for coefficient in COS[-2::-1]:
+            value = value * square + coefficient
+        packed = (value * math.sqrt(2.0 / TOTAL_FEATS)).astype(BF16)
+        return lax.dot_general(
+            packed, pw[...], (((1,), (1,)), ((), ())), preferred_element_type=F32
+        )
+
+    out = prior_share(left_side(xt[...]))
+    for i in range(NC):
+        pts[i] = jnp.where(low, out[64 * i : 64 * i + 32], out[64 * i + 32 : 64 * i + 64])
+
+    for copy in inputs[5:]:
+        copy.wait()
+
     mine = xt[:, pl.ds(pl.multiple_of((c // 2) * 128, 128), 128)]
     mine = jnp.where(lax.rem(c, 2) == 1, swap(mine), mine)
     xls[...] = mine
@@ -149,36 +194,10 @@
     xcs[...] = cand
     xcb[c] = cand
 
-    feat = pl.ds(pl.multiple_of(c * FEATS, FEATS), FEATS)
-    turn = 1.0 / (2.0 * math.pi)
-    zero = jnp.zeros((1, FEATS), F32)
-    bw[...] = right_side(
-        om[:, feat] * turn, rows8(zero, zero, zero, *split3(ph[:, feat] * turn))
-    )
-    pwd[...] = jnp.concatenate([pw[...], pw[...]], axis=1)
-    atb[...] = left_side(xt[...])
-
-    def feature_rows(left, first, count):
-        turns = jnp.dot(left[pl.ds(first, count), :], bw[...], preferred_element_type=F32)
-        part = turns - jnp.floor(turns + 0.5)
-        square = part * part
-        value = jnp.full(square.shape, COS[-1], F32)
-        for coefficient in COS[-2::-1]:
-            value = value * square + coefficient
-        packed = (value * math.sqrt(2.0 / TOTAL_FEATS)).astype(BF16)
-        return jnp.dot(packed, pwd[...], preferred_element_type=F32)
-
-    def train_features(i, carry):
-        out = feature_rows(atb, pl.multiple_of(i * OWN, OWN), OWN)
-        pts[i] = jnp.where(low, out[0:32], out[32:64])
-        return carry
-
-    lax.fori_loop(0, NC, train_features, 0)
-
     pl.semaphore_wait(barrier, NP - 1 + NZ - 1)
+    push(3, NC, cand_peer, lambda k: pts.at[cand_index(k)], ptb.at[c])
     push(0, NH, block_peer, lambda k: xt, xp.at[h])
     push(1, NZ, line_peer, lambda k: xls, xl.at[z])
-    push(3, NC, cand_peer, lambda k: pts.at[cand_index(k)], ptb.at[c])
     push(2, NC, cand_peer, lambda k: xcs, xcb.at[c])
     ptb[c] = pts[c]
 
@@ -216,18 +235,9 @@
             by[:, start : start + 256] = right_side(points, tail)
 
     def entries(first, count):
-        def one(j, carry):
-            columns = pl.ds(pl.multiple_of(j * 256, 256), 256)
-            power = jnp.dot(atl[pl.ds(first, count), :], by[:, columns], preferred_element_type=F32)
-            km[pl.ds(first, count), columns] = jnp.exp(power).astype(BF16)
-            return carry
-
-        lax.fori_loop(0, 8, one, 0)
-
-    arrived(1, xl)
-    for j in range(4):
-        atl[j * 128 : j * 128 + 128, :] = left_side(pair(xl[2 * j], xl[2 * j + 1]))
-    entries(0, 256)
+        rows = pl.ds(first, count)
+        power = jnp.dot(atl[rows, :], by[...], preferred_element_type=F32)
+        km[rows, :] = jnp.exp(power).astype(BF16)
 
     arrived(3, ptb)
     r0 = base - jnp.sum(ptb[...], axis=0)
@@ -239,111 +249,133 @@
     push(5, NZ, line_peer, lambda k: own0, r0l.at[z])
     rr_own = fold(r0 * r0)
 
-    entries(256, 256)
+    arrived(1, xl)
+    for j in range(4):
+        atl[j * 128 : j * 128 + 128, :] = left_side(pair(xl[2 * j], xl[2 * j + 1]))
+    entries(0, 512)
     entries(512, 256)
 
-    arrived(2, xcb)
-    for j in range(2):
-        joined = xcb[4 * j]
-        for g in range(1, 4):
-            joined = jnp.where(lane < 32 * g, joined, pltpu.roll(xcb[4 * j + g], 32 * g, 1))
-        atc[j * 128 : j * 128 + 128, :] = left_side(joined)
-
-    def cand_features(i, carry):
-        out = feature_rows(atc, pl.multiple_of(i * OWN, OWN), OWN)
-        pcs[2 * i] = jnp.where(low, out[0:16], out[16:32])
-        pcs[2 * i + 1] = jnp.where(low, out[32:48], out[48:64])
-        return carry
-
-    lax.fori_loop(0, 4, cand_features, 0)
-    push(6, NC, cand_peer, lambda k: pcs.at[cand_index(k)], pcb.at[c])
-    pcb[c] = pcs[c]
-
-    def product(field, pieces, cand_pieces):
+    def multiply(first, count, field):
+        rows = pl.ds(first, count)
         values = field[...].reshape(NP * 32, 128)
-        o1[...] = jnp.dot(km[:, 0:1024], values, preferred_element_type=F32)
-        o2[...] = jnp.dot(km[:, 1024:2048], values, preferred_element_type=F32)
-
-        def joined(first, size):
-            a1, b1 = o1[pl.ds(first, size), :], o1[pl.ds(first + size, size), :]
-            a2, b2 = o2[pl.ds(first, size), :], o2[pl.ds(first + size, size), :]
-            return jnp.where(low, a1, b2) + swap(jnp.where(low, b1, a2))
-
+        o1[rows, :] = jnp.dot(km[rows, 0:1024], values, preferred_element_type=F32)
+        o2[rows, :] = jnp.dot(km[rows, 1024:2048], values, preferred_element_type=F32)
+
+    def joined(first, size):
+        a1, b1 = o1[pl.ds(first, size), :], o1[pl.ds(first + size, size), :]
+        a2, b2 = o2[pl.ds(first, size), :], o2[pl.ds(first + size, size), :]
+        return jnp.where(low, a1, b2) + swap(jnp.where(low, b1, a2))
+
+    def train_product(pieces, field):
+        multiply(0, 512, field)
         for i in range(NZ):
             pieces[i] = joined(i * 64, 32)
+
+    def cand_product(pieces, field):
+        multiply(512, 256, field)
         for i in range(NZ):
-            cand_pieces[i] = joined(512 + i * 32, 16)
+            pieces[i] = joined(512 + i * 32, 16)
+
+    def ratio(part):
+        other = swap(part)
+        norms = jnp.where(low, other, part)
+        return norms, jnp.where(low, part, other) / norms + NOISE_LEVEL
 
     arrived(4, vb0)
-    product(vb0, kr, ucs)
+    train_product(kr, vb0)
     push(7, NZ, line_peer, lambda k: kr.at[line_index(k)], krb.at[z])
-    krb[z] = kr[z]
     arrived(5, r0l)
     curve = fold(jnp.sum(kr[...] * r0l[...], axis=0))
     part = jnp.where(low, curve, rr_own)
     sa_s[...] = part
     sa[q] = part
     push(8, NP, plane_peer, lambda k: sa_s, sa.at[q])
-    push(9, NZ, line_peer, lambda k: ucs.at[line_index(k)], ucb.at[z])
-    ucb[z] = ucs[z]
+    krb[z] = kr[z]
+    cand_product(ucs, vb0)
+
+    arrived(2, xcb)
+    tiles = []
+    for j in range(2):
+        tile = xcb[4 * j]
+        for g in range(1, 4):
+            tile = jnp.where(lane < 32 * g, tile, pltpu.roll(xcb[4 * j + g], 32 * g, 1))
+        tiles.append(tile)
+    out = prior_share(left_side(jnp.concatenate(tiles, axis=1)))
+    for i in range(NC):
+        pcs[i] = jnp.where(low, out[32 * i : 32 * i + 16], out[32 * i + 16 : 32 * i + 32])
+    pcb[c] = pcs[c]
+
     arrived(8, sa)
     part = jnp.sum(sa[...], axis=0)
     sb_s[...] = part
     sb[z] = part
     push(10, NZ, line_peer, lambda k: sb_s, sb.at[z])
+    share = ratio(part)[1]
     arrived(7, krb)
     r0 = own0[...]
     image = jnp.sum(krb[...], axis=0) + NOISE_LEVEL * r0
+
+    own1[...] = image
+    q0l[z] = image
+    high = (image - share * r0).astype(BF16)
+    hb1[...] = high
+    vb1[q] = high
+    push(11, NP, plane_peer, lambda k: hb1, vb1.at[q])
+    push(12, NZ, line_peer, lambda k: own1, q0l.at[z])
     arrived(10, sb)
-    part = jnp.sum(sb[...], axis=0)
-    other = swap(part)
-    rr0 = jnp.where(low, other, part)
-    alpha1 = rr0 / (jnp.where(low, part, other) + NOISE_LEVEL * rr0)
+    rr0, quotient = ratio(jnp.sum(sb[...], axis=0))
+    alpha1 = 1.0 / quotient
     r1 = r0 - alpha1 * image
-
-    own1[...] = r1
-    r1l[z] = r1
-    hb1[...] = r1.astype(BF16)
-    vb1[q] = r1.astype(BF16)
-    push(11, NP, plane_peer, lambda k: hb1, vb1.at[q])
     rr1_own = fold(r1 * r1)
     ra_s[...] = rr1_own
     ra[q] = rr1_own
     push(13, NP, plane_peer, lambda k: ra_s, ra.at[q])
-    push(12, NZ, line_peer, lambda k: own1, r1l.at[z])
+    push(9, NZ, line_peer, lambda k: ucs.at[line_index(k)], ucb.at[z])
+    ucb[z] = ucs[z]
+    push(6, NC, cand_peer, lambda k: pcs.at[cand_index(k)], pcb.at[c])
+    mixed_own = fold(r0 * r1)
+    arrived(11, vb1)
+    train_product(kq, vb1)
+    arrived(12, q0l)
+    r1l = r0l[...] - alpha1 * q0l[...]
+    k1 = (1.0 - alpha1 * share) * kr[...] - alpha1 * kq[...]
+    curve = fold(jnp.sum(r1l * k1, axis=0)) + NOISE_LEVEL * rr1_own
+    mixed = fold(jnp.sum(r0l[...] * k1 + r1l * kr[...], axis=0)) + 2.0 * NOISE_LEVEL * mixed_own
+    part = jnp.where(low, curve, mixed)
+    qa_s[...] = part
+    qa[q] = part
+    push(16, NP, plane_peer, lambda k: qa_s, qa.at[q])
     arrived(13, ra)
     part = jnp.sum(ra[...], axis=0)
     rb_s[...] = part
     rb[z] = part
     push(14, NZ, line_peer, lambda k: rb_s, rb.at[z])
-    arrived(11, vb1)
-    product(vb1, kr1, vcs)
-    push(15, NZ, line_peer, lambda k: vcs.at[line_index(k)], vcb.at[z])
-    vcb[z] = vcs[z]
-    arrived(12, r1l)
-    arrived(14, rb)
-    rr1 = jnp.sum(rb[...], axis=0)
-    beta = rr1 / rr0
-    curve = fold(jnp.sum((r1l[...] + beta * r0l[...]) * (kr1[...] + beta * kr[...]), axis=0))
-    r0, r1 = own0[...], own1[...]
-    d1 = r1 + beta * r0
-    part = curve + NOISE_LEVEL * fold(d1 * d1)
-    qa_s[...] = part
-    qa[q] = part
-    push(16, NP, plane_peer, lambda k: qa_s, qa.at[q])
-    arrived(6, pcb)
-    prior = jnp.sum(pcb[...], axis=0)
-    arrived(9, ucb)
-    first_part = jnp.sum(ucb[...], axis=0)
+    cand_product(wcs, vb1)
+    wcs[...] = wcs[...] + share * ucs[...]
+    push(15, NZ, line_peer, lambda k: wcs.at[line_index(k)], wcb.at[z])
+    wcb[z] = wcs[z]
     arrived(16, qa)
     part = jnp.sum(qa[...], axis=0)
     qb_s[...] = part
     qb[z] = part
     push(17, NZ, line_peer, lambda k: qb_s, qb.at[z])
-    arrived(15, vcb)
-    second_part = jnp.sum(vcb[...], axis=0)
+    arrived(6, pcb)
+    prior = jnp.sum(pcb[...], axis=0)
+    arrived(9, ucb)
+    first_part = jnp.sum(ucb[...], axis=0)
+    arrived(14, rb)
+    rr1 = jnp.sum(rb[...], axis=0)
+    beta = rr1 / rr0
+    arrived(15, wcb)
+    second_part = first_part - alpha1 * jnp.sum(wcb[...], axis=0)
+    r0 = own0[...]
+    r1 = r0 - alpha1 * own1[...]
+    d1 = r1 + beta * r0
     arrived(17, qb)
-    alpha2 = rr1 / jnp.sum(qb[...], axis=0)
+    part = jnp.sum(qb[...], axis=0)
+    other = swap(part)
+    curve, mixed = jnp.where(low, part, other), jnp.where(low, other, part)
+    alpha2 = rr1 / (curve + beta * (mixed + beta * (rr0 / alpha1)))
 
     result = alpha1 * r0 + alpha2 * d1
     sol[0:32, :] = result[:, 0:64]
@@ -353,7 +385,7 @@
     sam[16:32, :] = swap(result)[:, 0:64]
 
     for phase, buf in enumerate(
-        (xp, xl, xcb, ptb, vb0, r0l, pcb, krb, sa, ucb, sb, vb1, r1l, ra, rb, vcb, qa, qb)
+        (xp, xl, xcb, ptb, vb0, r0l, pcb, krb, sa, ucb, sb, vb1, q0l, ra, rb, wcb, qa, qb)
     ):
         settle(phase, ssem, buf)
 
@@ -363,20 +395,22 @@
     field = lambda n, rows, dtype=F32: vmem((n, rows, 128), dtype)
     tile, row = vmem((8, 128), F32), vmem((1, 128), F32)
     scratch = [
+        vmem((8, 512), F32), vmem((8, 1024), F32), vmem((1, OWN), F32), vmem((OWN, OWN), F32),
+        vmem((8, FEATS), F32), vmem((1, FEATS), F32), vmem((2 * OWN, FEATS), BF16),
         tile, field(NZ, 8), tile, field(NC, 8), vmem((NH, 8, 512), F32),
-        vmem((128, 2048), BF16), vmem((128, FEATS), BF16), vmem((512, 128), BF16),
-        vmem((256, 128), BF16), vmem((768, 128), BF16), vmem((768, 2048), BF16),
-        vmem((FEATS, 128), BF16),
+        vmem((128, 2048), BF16), vmem((128, FEATS), BF16), vmem((768, 128), BF16), vmem((768, 2048), BF16),
         field(NC, 32), field(NC, 32), field(NC, 16), field(NC, 16),
         vmem((32, 128), F32), vmem((32, 128), F32),
-        field(NP, 32, BF16), field(NP, 32, BF16), field(NZ, 32), field(NZ, 32),
+        field(NP, 32, BF16), field(NP, 32, BF16),
+        field(NZ, 32), field(NZ, 32),
         vmem((768, 128), F32), vmem((768, 128), F32),
         field(NZ, 32), field(NZ, 32), field(NZ, 32),
         field(NZ, 16), field(NZ, 16), field(NZ, 16), field(NZ, 16),
         row, field(NP, 1), row, field(NZ, 1), row, field(NP, 1), row, field(NZ, 1),
         row, field(NP, 1), row, field(NZ, 1),
         vmem((32, 128), BF16), vmem((32, 128), BF16),
-        pltpu.SemaphoreType.DMA((18,)), pltpu.SemaphoreType.DMA((18,)),
+        pltpu.SemaphoreType.DMA((8,)), pltpu.SemaphoreType.DMA((18,)),
+        pltpu.SemaphoreType.DMA((18,)),
     ]
     return pl.pallas_call(
         kernel,
@@ -384,15 +418,15 @@
             jax.ShapeDtypeStruct((CANDS, OWN), F32),
             jax.ShapeDtypeStruct((OWN, OWN), F32),
         ),
-        in_specs=[pl.BlockSpec(memory_space=vmem)] * 7,
+        in_specs=[pl.BlockSpec(memory_space=pltpu.HBM)] * 7,
         out_specs=(pl.BlockSpec(memory_space=vmem),) * 2,
         scratch_shapes=scratch,
         compiler_params=pltpu.CompilerParams(
-            collective_id=0, has_side_effects=True, vmem_limit_bytes=32 * 1024 * 1024
+            collective_id=0, has_side_effects=True, vmem_limit_bytes=64 * 1024 * 1024
         ),
     )(
         x_train, x_cand, targets.reshape(1, OWN), noise, omega,
-        phase.reshape(1, TOTAL_FEATS), prior_weights,
+        phase.reshape(1, TOTAL_FEATS), prior_weights.T,
     )
 
 

time: 58.7 us -> 49.3 us (0.84)
  Pallas kernels: 54 us -> 46.5 us
  local copies, waits for them, and re-layouts: 3.69 us -> 1.95 us
    pallas_call x1, Pallas kernels: 54 us -> 46.5 us  [body(): pl.pallas_call(kernel, out_shape=(jax.ShapeDtypeStruct((CANDS, OWN), F32)...]
    unnamed x15 -> x4, local copies, waits for them, and re-layouts: 3.69 us -> 1.95 us
where the time goes in v2:
time: 49.3 us; the launch traced here: 49.1 us
  Pallas kernels  46.5 us (94%)
  local copies, waits for them, and re-layouts  1.95 us (4%)
  between operations  0.65 us (1%)
    pallas_call x1, Pallas kernels, body(): pl.pallas_call(kernel, out_shape=(jax.ShapeDtypeStruct((CANDS, OWN), F32)...  46.5 us
    unnamed x4, local copies, waits for them, and re-layouts  1.95 us

profile of v2, /device:TPU:1, one launch (start us, length us, event | category | flops | bytes accessed | tf_op | source)
XLA Modules:
  0.0 49.1 jit_solution(5347859804379969704)
XLA Ops:
  0.6 46.5 %shard_map.86 = (f32[32,64]{1,0:T(8,128)}, f32[64,64]{1,0:T(8,128)}) custom-call(f32[8,512]{1,0:T(8,128)} %xt_hbm.1, f32[8,1024]{1,0:T(8,128)} %xc_hbm.1, f32[1,64]{1,0:T(1,128)} %bitcast.5, f32[64,64]{1,0:T(8,128)} %nz_hbm.1, f32[8,4096]{1,0:T(8,128)} %om_hbm.1, f32[1,4096]{1,0:T(1,128)} %bitcast.4, bf16[64,512]{1,0:T(8,128)(2,1)} %bitcast.3), custom_call_target="tpu_custom_call" | custom-call | tf_op jit(solution)/shard_map/pallas_call | solution.py:415
  47.2 0.0 copy-start
  47.2 1.3 %copy.11 = f32[32,64]{1,0:T(8,128)} copy(f32[32,64]{1,0:T(8,128)} %get-tuple-element.4) | data formatting | bytes 16384
  48.5 0.0 copy-done
  48.5 0.6 %copy.12 = f32[64,64]{1,0:T(8,128)} copy(f32[64,64]{1,0:T(8,128)S(1)} %copy-done) | data formatting | bytes 32768
Async XLA Ops:
  47.2 1.3 %copy-start = (f32[64,64]{1,0:T(8,128)S(1)}, f32[64,64]{1,0:T(8,128)}, u32[]{:S(2)}) copy-start(f32[64,64]{1,0:T(8,128)} %get-tuple-element.5) | copy-start | bytes 49156

commit v3 on v2

--- a/solution.py
+++ b/solution.py
@@ -73,26 +73,37 @@
     h = y_hi * 2 + core
     q = h * NC + c
 
-    def plane_peer(k):
-        other = lax.rem(q + k, NP)
-        oh, oc = other // NC, lax.rem(other, NC)
-        return ((oh // 2) * 16 + z * 2 + lax.rem(oh, 2), oc)
-
-    def line_index(k):
-        return lax.rem(z + k, NZ)
-
-    def line_peer(k):
-        return (y_hi * 16 + line_index(k) * 2 + core, c)
-
-    def cand_index(k):
-        return lax.rem(c + k, NC)
-
-    def cand_peer(k):
-        return (t, cand_index(k))
-
-    def block_peer(k):
-        oh = lax.rem(h + k, NH)
-        return ((oh // 2) * 16 + z * 2 + lax.rem(oh, 2), c)
+    x, y = c // 2, y_hi * 2 + lax.rem(c, 2)
+
+    ys = [lax.rem(y + k, 4) for k in range(4)]
+    xs = [lax.rem(x + k, 4) for k in range(4)]
+    cores = [core, 1 - core]
+    hops = lambda k, n: min(k, n - k)
+
+    def device(dx, dy, dz, dcore):
+        other_z = z if dz == 0 else lax.rem(z + dz, NZ)
+        return (
+            (ys[dy] // 2) * 16 + other_z * 2 + cores[dcore],
+            xs[dx] * 2 + lax.rem(ys[dy], 2),
+        )
+
+    def ranked(group):
+        return sorted(group, key=lambda d: -(hops(d[0], 4) + hops(d[1], 4) + hops(d[2], NZ)))
+
+    plane = [
+        device(*d)
+        for d in ranked((i, j, 0, k) for i in range(4) for j in range(4) for k in range(2))
+        if d != (0, 0, 0, 0)
+    ]
+    plane = [(peer, None) for peer in plane]
+    line = [
+        (device(0, 0, k, 0), lax.rem(z + k, NZ)) for k in (4, 3, 5, 2, 6, 1, 7)
+    ]
+    cands = [
+        ((t, xs[i] * 2 + lax.rem(y + j, 2)), xs[i] * 2 + lax.rem(y + j, 2))
+        for i, j in ((2, 1), (2, 0), (1, 1), (3, 1), (1, 0), (3, 0), (0, 1))
+    ]
+    blocks = [(device(0, j, 0, k), None) for j, k in ((2, 1), (2, 0), (0, 1))]
 
     feat = pl.ds(pl.multiple_of(c * FEATS, FEATS), FEATS)
     inputs = [
@@ -115,29 +126,19 @@
 
     barrier = pltpu.get_barrier_semaphore()
 
-    def greet(peer, count):
-        def one(k, carry):
-            pl.semaphore_signal(barrier, inc=1, device_id=peer(k), device_id_type=MESH)
-            return carry
-
-        lax.fori_loop(1, count, one, 0)
-
-    greet(plane_peer, NP)
-    greet(line_peer, NZ)
-
-    def push(phase, count, peer, source, target):
-        def one(k, carry):
+    for peer, _ in plane + line:
+        pl.semaphore_signal(barrier, inc=1, device_id=peer, device_id_type=MESH)
+
+    def push(phase, peers, source, target):
+        for peer, index in peers:
             pltpu.make_async_remote_copy(
-                src_ref=source(k),
+                src_ref=source if index is None else source(index),
                 dst_ref=target,
                 send_sem=ssem.at[phase],
                 recv_sem=rsem.at[phase],
-                device_id=peer(k),
+                device_id=peer,
                 device_id_type=MESH,
             ).start()
-            return carry
-
-        lax.fori_loop(1, count, one, 0)
 
     def settle(phase, sems, buf):
         ref = buf.at[pl.ds(0, buf.shape[0] - 1)]
@@ -181,6 +182,8 @@
     for i in range(NC):
         pts[i] = jnp.where(low, out[64 * i : 64 * i + 32], out[64 * i + 32 : 64 * i + 64])
 
+    pl.semaphore_wait(barrier, NP - 1 + NZ - 1)
+    push(3, cands, lambda i: pts.at[i], ptb.at[c])
     for copy in inputs[5:]:
         copy.wait()
 
@@ -193,12 +196,9 @@
     cand = pltpu.roll(cand, lax.rem(128 - lax.rem(t, 4) * 32, 128), 1)
     xcs[...] = cand
     xcb[c] = cand
-
-    pl.semaphore_wait(barrier, NP - 1 + NZ - 1)
-    push(3, NC, cand_peer, lambda k: pts.at[cand_index(k)], ptb.at[c])
-    push(0, NH, block_peer, lambda k: xt, xp.at[h])
-    push(1, NZ, line_peer, lambda k: xls, xl.at[z])
-    push(2, NC, cand_peer, lambda k: xcs, xcb.at[c])
+    push(0, blocks, xt, xp.at[h])
+    push(1, line, lambda i: xls, xl.at[z])
+    push(2, cands, lambda i: xcs, xcb.at[c])
     ptb[c] = pts[c]
 
     row = tg[...]
@@ -245,8 +245,8 @@
     r0l[z] = r0
     hb0[...] = r0.astype(BF16)
     vb0[q] = r0.astype(BF16)
-    push(4, NP, plane_peer, lambda k: hb0, vb0.at[q])
-    push(5, NZ, line_peer, lambda k: own0, r0l.at[z])
+    push(4, plane, hb0, vb0.at[q])
+    push(5, line, lambda i: own0, r0l.at[z])
     rr_own = fold(r0 * r0)
 
     arrived(1, xl)
@@ -283,13 +283,13 @@
 
     arrived(4, vb0)
     train_product(kr, vb0)
-    push(7, NZ, line_peer, lambda k: kr.at[line_index(k)], krb.at[z])
+    push(7, line, lambda i: kr.at[i], krb.at[z])
     arrived(5, r0l)
     curve = fold(jnp.sum(kr[...] * r0l[...], axis=0))
     part = jnp.where(low, curve, rr_own)
     sa_s[...] = part
     sa[q] = part
-    push(8, NP, plane_peer, lambda k: sa_s, sa.at[q])
+    push(8, plane, sa_s, sa.at[q])
     krb[z] = kr[z]
     cand_product(ucs, vb0)
 
@@ -309,8 +309,9 @@
     part = jnp.sum(sa[...], axis=0)
     sb_s[...] = part
     sb[z] = part
-    push(10, NZ, line_peer, lambda k: sb_s, sb.at[z])
-    share = ratio(part)[1]
+    push(10, line, lambda i: sb_s, sb.at[z])
+    norms, quotient = ratio(part)
+    share = jnp.where(norms > 0.0, quotient, 0.0)
     arrived(7, krb)
     r0 = own0[...]
     image = jnp.sum(krb[...], axis=0) + NOISE_LEVEL * r0
@@ -320,8 +321,8 @@
     high = (image - share * r0).astype(BF16)
     hb1[...] = high
     vb1[q] = high
-    push(11, NP, plane_peer, lambda k: hb1, vb1.at[q])
-    push(12, NZ, line_peer, lambda k: own1, q0l.at[z])
+    push(11, plane, hb1, vb1.at[q])
+    push(12, line, lambda i: own1, q0l.at[z])
     arrived(10, sb)
     rr0, quotient = ratio(jnp.sum(sb[...], axis=0))
     alpha1 = 1.0 / quotient
@@ -329,10 +330,10 @@
     rr1_own = fold(r1 * r1)
     ra_s[...] = rr1_own
     ra[q] = rr1_own
-    push(13, NP, plane_peer, lambda k: ra_s, ra.at[q])
-    push(9, NZ, line_peer, lambda k: ucs.at[line_index(k)], ucb.at[z])
+    push(13, plane, ra_s, ra.at[q])
+    push(9, line, lambda i: ucs.at[i], ucb.at[z])
     ucb[z] = ucs[z]
-    push(6, NC, cand_peer, lambda k: pcs.at[cand_index(k)], pcb.at[c])
+    push(6, cands, lambda i: pcs.at[i], pcb.at[c])
     mixed_own = fold(r0 * r1)
     arrived(11, vb1)
     train_product(kq, vb1)
@@ -344,21 +345,21 @@
     part = jnp.where(low, curve, mixed)
     qa_s[...] = part
     qa[q] = part
-    push(16, NP, plane_peer, lambda k: qa_s, qa.at[q])
+    push(16, plane, qa_s, qa.at[q])
     arrived(13, ra)
     part = jnp.sum(ra[...], axis=0)
     rb_s[...] = part
     rb[z] = part
-    push(14, NZ, line_peer, lambda k: rb_s, rb.at[z])
+    push(14, line, lambda i: rb_s, rb.at[z])
     cand_product(wcs, vb1)
     wcs[...] = wcs[...] + share * ucs[...]
-    push(15, NZ, line_peer, lambda k: wcs.at[line_index(k)], wcb.at[z])
+    push(15, line, lambda i: wcs.at[i], wcb.at[z])
     wcb[z] = wcs[z]
     arrived(16, qa)
     part = jnp.sum(qa[...], axis=0)
     qb_s[...] = part
     qb[z] = part
-    push(17, NZ, line_peer, lambda k: qb_s, qb.at[z])
+    push(17, line, lambda i: qb_s, qb.at[z])
     arrived(6, pcb)
     prior = jnp.sum(pcb[...], axis=0)
     arrived(9, ucb)
@@ -412,6 +413,10 @@
         pltpu.SemaphoreType.DMA((8,)), pltpu.SemaphoreType.DMA((18,)),
         pltpu.SemaphoreType.DMA((18,)),
     ]
+    operands = (
+        x_train, x_cand, targets.reshape(1, OWN), noise, omega,
+        phase.reshape(1, TOTAL_FEATS), prior_weights.T,
+    )
     return pl.pallas_call(
         kernel,
         out_shape=(
@@ -422,12 +427,9 @@
         out_specs=(pl.BlockSpec(memory_space=vmem),) * 2,
         scratch_shapes=scratch,
         compiler_params=pltpu.CompilerParams(
-            collective_id=0, has_side_effects=True, vmem_limit_bytes=64 * 1024 * 1024
+            collective_id=0, has_side_effects=True, vmem_limit_bytes=32 * 1024 * 1024
         ),
-    )(
-        x_train, x_cand, targets.reshape(1, OWN), noise, omega,
-        phase.reshape(1, TOTAL_FEATS), prior_weights.T,
-    )
+    )(*(pltpu.with_memory_space_constraint(value, pltpu.HBM) for value in operands))
 
 
 def solution(mesh):

time: 49.3 us -> 44.4 us (0.901)
  Pallas kernels: 46.5 us -> 42.4 us
  local copies, waits for them, and re-layouts: 1.95 us -> 1.22 us
    pallas_call x1, Pallas kernels: 46.5 us -> 42.4 us  [body(): pl.pallas_call(kernel, out_shape=(jax.ShapeDtypeStruct((CANDS, OWN), F32)...]
    unnamed x4 -> x2, local copies, waits for them, and re-layouts: 1.95 us -> 1.22 us
where the time goes in v3:
time: 44.4 us; the launch traced here: 44.2 us
  Pallas kernels  42.4 us (95%)
  local copies, waits for them, and re-layouts  1.22 us (3%)
  between operations  0.64 us (1%)
    pallas_call x1, Pallas kernels, body(): pl.pallas_call(kernel, out_shape=(jax.ShapeDtypeStruct((CANDS, OWN), F32)...  42.4 us
    unnamed x2, local copies, waits for them, and re-layouts  1.22 us

profile of v3, /device:TPU:1, one launch (start us, length us, event | category | flops | bytes accessed | tf_op | source)
XLA Modules:
  0.0 44.2 jit_solution(188765738380004691)
XLA Ops:
  0.6 42.4 %shard_map.86 = (f32[32,64]{1,0:T(8,128)S(1)}, f32[64,64]{1,0:T(8,128)S(1)}) custom-call(f32[8,512]{1,0:T(8,128)} %xt_hbm.1, f32[8,1024]{1,0:T(8,128)} %xc_hbm.1, f32[1,64]{1,0:T(1,128)} %bitcast.5, f32[64,64]{1,0:T(8,128)} %nz_hbm.1, f32[8,4096]{1,0:T(8,128)} %om_hbm.1, f32[1,4096]{1,0:T(1,128)} %bitcast.4, bf16[64,512]{1,0:T(8,128)(2,1)} %bitcast.3), custom_call_target="tpu_custom_call" | custom-call | tf_op jit(solution)/shard_map/pallas_call | solution.py:420
  43.0 0.6 %copy.11 = f32[32,64]{1,0:T(8,128)} copy(f32[32,64]{1,0:T(8,128)S(1)} %get-tuple-element.4) | data formatting | bytes 16384
  43.6 0.6 %copy.12 = f32[64,64]{1,0:T(8,128)} copy(f32[64,64]{1,0:T(8,128)S(1)} %get-tuple-element.5) | data formatting | bytes 32768

commit v4 on v3

--- a/solution.py
+++ b/solution.py
@@ -16,14 +16,21 @@
 FEATS = 512
 TOTAL_FEATS = 4096
 NOISE_LEVEL = 0.5
-COS = (
-    0.9999999890590217,
-    -19.73920449945381,
-    64.93911745989173,
-    -85.45013953082398,
-    60.16763095051855,
-    -25.967599246994247,
-    6.528658159389057,
+PLANE_ORDER = sorted(
+    ((i, j, k) for i in range(4) for j in range(4) for k in range(2) if i + j + k),
+    key=lambda d: -(min(d[0], 4 - d[0]) + min(d[1], 4 - d[1])),
+)
+LINE_ORDER = (4, 3, 5, 2, 6, 1, 7, 0)
+
+
+def place_of(k):
+    return LINE_ORDER.index(k % NZ)
+SIN = (
+    6.283185159611151,
+    -41.3416549293423,
+    81.60099819256979,
+    -76.5496568198889,
+    39.53581370662112,
 )
 
 
@@ -60,7 +67,7 @@
 
 
 def kernel(
-    xt_hbm, xc_hbm, tg_hbm, nz_hbm, om_hbm, ph_hbm, pw_hbm, sam, sol,
+    xt_hbm, xc_hbm, tg_hbm, nz_hbm, om_hbm, ph_hbm, pw_hbm, packed,
     xt, xc, tg, nz, om, ph, pw,
     xls, xl, xcs, xcb, xp, by, bw, atl, km,
     pts, ptb, pcs, pcb, own0, own1, vb0, vb1, r0l, q0l,
@@ -75,35 +82,27 @@
 
     x, y = c // 2, y_hi * 2 + lax.rem(c, 2)
 
+    y_lo = lax.rem(c, 2)
     ys = [lax.rem(y + k, 4) for k in range(4)]
     xs = [lax.rem(x + k, 4) for k in range(4)]
+    zs = [lax.rem(z + k, NZ) for k in range(NZ)]
     cores = [core, 1 - core]
-    hops = lambda k, n: min(k, n - k)
 
     def device(dx, dy, dz, dcore):
-        other_z = z if dz == 0 else lax.rem(z + dz, NZ)
         return (
-            (ys[dy] // 2) * 16 + other_z * 2 + cores[dcore],
+            (ys[dy] // 2) * 16 + zs[dz] * 2 + cores[dcore],
             xs[dx] * 2 + lax.rem(ys[dy], 2),
         )
 
-    def ranked(group):
-        return sorted(group, key=lambda d: -(hops(d[0], 4) + hops(d[1], 4) + hops(d[2], NZ)))
-
-    plane = [
-        device(*d)
-        for d in ranked((i, j, 0, k) for i in range(4) for j in range(4) for k in range(2))
-        if d != (0, 0, 0, 0)
+    plane = [(device(i, j, 0, k), i) for i, j, k in PLANE_ORDER]
+    line = [(device(0, 0, k, 0), k) for k in LINE_ORDER[:-1]]
+    blocks = [(device(0, j, 0, k), None) for j, k in ((2, 1), (2, 0), (0, 1))]
+    near = 1 - y_lo
+    cands = [
+        ((t, xs[i] * 2 + j), (i, j))
+        for i, j in ((2, 0), (2, 1), (1, 0), (1, 1), (3, 0), (3, 1), (0, near))
     ]
-    plane = [(peer, None) for peer in plane]
-    line = [
-        (device(0, 0, k, 0), lax.rem(z + k, NZ)) for k in (4, 3, 5, 2, 6, 1, 7)
-    ]
-    cands = [
-        ((t, xs[i] * 2 + lax.rem(y + j, 2)), xs[i] * 2 + lax.rem(y + j, 2))
-        for i, j in ((2, 1), (2, 0), (1, 1), (3, 1), (1, 0), (3, 0), (0, 1))
-    ]
-    blocks = [(device(0, j, 0, k), None) for j, k in ((2, 1), (2, 0), (0, 1))]
+    sub = h * 2 + y_lo
 
     feat = pl.ds(pl.multiple_of(c * FEATS, FEATS), FEATS)
     inputs = [
@@ -121,31 +120,35 @@
             )
         )
     ]
-    for copy in inputs:
+    barrier = pltpu.get_barrier_semaphore()
+    for copy in inputs[:5]:
         copy.start()
-
-    barrier = pltpu.get_barrier_semaphore()
-
     for peer, _ in plane + line:
         pl.semaphore_signal(barrier, inc=1, device_id=peer, device_id_type=MESH)
+    for copy in inputs[5:]:
+        copy.start()
 
     def push(phase, peers, source, target):
-        for peer, index in peers:
+        for peer, tag in peers:
+            number = phase(tag) if callable(phase) else phase
             pltpu.make_async_remote_copy(
-                src_ref=source if index is None else source(index),
-                dst_ref=target,
-                send_sem=ssem.at[phase],
-                recv_sem=rsem.at[phase],
+                src_ref=source(tag) if callable(source) else source,
+                dst_ref=target(tag) if callable(target) else target,
+                send_sem=ssem.at[number],
+                recv_sem=rsem.at[number],
                 device_id=peer,
                 device_id_type=MESH,
             ).start()
 
-    def settle(phase, sems, buf):
-        ref = buf.at[pl.ds(0, buf.shape[0] - 1)]
+    def settle(phase, sems, buf, count=None):
+        ref = buf.at[pl.ds(0, count or buf.shape[0] - 1)]
         pltpu.make_async_copy(ref, ref, sems.at[phase]).wait()
 
-    def arrived(phase, buf):
-        settle(phase, rsem, buf)
+    def arrived(phase, buf, count=None):
+        settle(phase, rsem, buf, count)
+
+    def gather(base, source, target):
+        push(lambda i: base + -i % 4, plane, source, lambda i: target.at[(-i % 4) * 8 + sub])
 
     lane = lax.broadcasted_iota(jnp.int32, (1, 128), 1)
     low = lane < 64
@@ -168,12 +171,13 @@
     bw[...] = right_side(om[...] * turn, rows8(zero, zero, zero, *split3(ph[...] * turn)))
     def prior_share(left):
         turns = jnp.dot(left, bw[...], preferred_element_type=F32)
-        part = turns - jnp.floor(turns + 0.5)
-        square = part * part
-        value = jnp.full(square.shape, COS[-1], F32)
-        for coefficient in COS[-2::-1]:
-            value = value * square + coefficient
-        packed = (value * math.sqrt(2.0 / TOTAL_FEATS)).astype(BF16)
+        wave = jnp.abs(turns - jnp.floor(turns) - 0.5) - 0.25
+        square = wave * wave
+        scale = math.sqrt(2.0 / TOTAL_FEATS)
+        value = square * (SIN[-1] * scale) + SIN[-2] * scale
+        for coefficient in SIN[-3::-1]:
+            value = value * square + coefficient * scale
+        packed = (value * wave).astype(BF16)
         return lax.dot_general(
             packed, pw[...], (((1,), (1,)), ((), ())), preferred_element_type=F32
         )
@@ -181,24 +185,23 @@
     out = prior_share(left_side(xt[...]))
     for i in range(NC):
         pts[i] = jnp.where(low, out[64 * i : 64 * i + 32], out[64 * i + 32 : 64 * i + 64])
-
     pl.semaphore_wait(barrier, NP - 1 + NZ - 1)
-    push(3, cands, lambda i: pts.at[i], ptb.at[c])
+    push(3, cands, lambda tag: pts.at[xs[tag[0]] * 2 + tag[1]], ptb.at[c])
     for copy in inputs[5:]:
         copy.wait()
 
     mine = xt[:, pl.ds(pl.multiple_of((c // 2) * 128, 128), 128)]
     mine = jnp.where(lax.rem(c, 2) == 1, swap(mine), mine)
     xls[...] = mine
-    xl[z] = mine
+    xl[place_of(0)] = mine
     xp[h] = xt[...]
     cand = xc[:, pl.ds(pl.multiple_of((t // 4) * 128, 128), 128)]
     cand = pltpu.roll(cand, lax.rem(128 - lax.rem(t, 4) * 32, 128), 1)
     xcs[...] = cand
     xcb[c] = cand
     push(0, blocks, xt, xp.at[h])
-    push(1, line, lambda i: xls, xl.at[z])
-    push(2, cands, lambda i: xcs, xcb.at[c])
+    push(1, line, xls, lambda k: xl.at[place_of(-k)])
+    push(2, cands, xcs, xcb.at[c])
     ptb[c] = pts[c]
 
     row = tg[...]
@@ -220,16 +223,12 @@
         )
 
     arrived(0, xp)
-    for i in range(NH):
-        uppers, lowers = [], []
-        for j in range(2):
-            tiles = [xp[i, :, j * 256 + 128 * g : j * 256 + 128 * g + 128] for g in range(2)]
-            uppers.append(pair(*[jnp.where(lane < 32, a, pltpu.roll(a, 96, 1)) for a in tiles]))
-            lowers.append(
-                pair(*[jnp.where(lane < 32, pltpu.roll(a, 96, 1), swap(a)) for a in tiles])
-            )
-        for start, tiles in ((i * 256, uppers), (1024 + i * 256, lowers)):
-            points = jnp.concatenate(tiles, axis=1)
+    for i in range(4):
+        tiles = [xp[g, :, pl.ds(pl.multiple_of(xs[i] * 128, 128), 128)] for g in range(NH)]
+        uppers = [jnp.where(lane < 32, a, pltpu.roll(a, 96, 1)) for a in tiles]
+        lowers = [jnp.where(lane < 32, pltpu.roll(a, 96, 1), swap(a)) for a in tiles]
+        for start, halves in ((i * 256, uppers), (1024 + i * 256, lowers)):
+            points = jnp.concatenate([pair(*halves[:2]), pair(*halves[2:])], axis=1)
             ones = jnp.ones((1, 256), F32)
             tail = rows8(ones, ones, ones, *split3(half_norm(points)))
             by[:, start : start + 256] = right_side(points, tail)
@@ -242,11 +241,11 @@
     arrived(3, ptb)
     r0 = base - jnp.sum(ptb[...], axis=0)
     own0[...] = r0
-    r0l[z] = r0
+    r0l[place_of(0)] = r0
     hb0[...] = r0.astype(BF16)
-    vb0[q] = r0.astype(BF16)
-    push(4, plane, hb0, vb0.at[q])
-    push(5, line, lambda i: own0, r0l.at[z])
+    vb0[sub] = r0.astype(BF16)
+    gather(18, hb0, vb0)
+    push(5, line, own0, lambda k: r0l.at[place_of(-k)])
     rr_own = fold(r0 * r0)
 
     arrived(1, xl)
@@ -255,24 +254,38 @@
     entries(0, 512)
     entries(512, 256)
 
-    def multiply(first, count, field):
+    def group_product(first, count, field, i, fresh):
         rows = pl.ds(first, count)
-        values = field[...].reshape(NP * 32, 128)
-        o1[rows, :] = jnp.dot(km[rows, 0:1024], values, preferred_element_type=F32)
-        o2[rows, :] = jnp.dot(km[rows, 1024:2048], values, preferred_element_type=F32)
+        values = field[8 * i : 8 * i + 8].reshape(256, 128)
+        for start, out in ((0, o1), (1024, o2)):
+            term = jnp.dot(
+                km[rows, start + 256 * i : start + 256 * i + 256],
+                values,
+                preferred_element_type=F32,
+            )
+            out[rows, :] = term if fresh else out[rows, :] + term
 
     def joined(first, size):
         a1, b1 = o1[pl.ds(first, size), :], o1[pl.ds(first + size, size), :]
         a2, b2 = o2[pl.ds(first, size), :], o2[pl.ds(first + size, size), :]
         return jnp.where(low, a1, b2) + swap(jnp.where(low, b1, a2))
 
-    def train_product(pieces, field):
-        multiply(0, 512, field)
-        for i in range(NZ):
-            pieces[i] = joined(i * 64, 32)
+    def train_product(pieces, base, field, ready):
+        for i in range(4):
+            arrived(base + i, field, 7 if i == 0 else 8)
+        values = field[...].reshape(NP * 32, 128)
+        for first in (0, 4):
+            rows = pl.ds(64 * first, 256)
+            o1[rows, :] = jnp.dot(km[rows, 0:1024], values, preferred_element_type=F32)
+            o2[rows, :] = jnp.dot(km[rows, 1024:2048], values, preferred_element_type=F32)
+            for k in range(first, first + 4):
+                pieces[k] = joined(64 * k, 32)
+            ready(first)
 
     def cand_product(pieces, field):
-        multiply(512, 256, field)
+        values = field[...].reshape(NP * 32, 128)
+        o1[512:768, :] = jnp.dot(km[512:768, 0:1024], values, preferred_element_type=F32)
+        o2[512:768, :] = jnp.dot(km[512:768, 1024:2048], values, preferred_element_type=F32)
         for i in range(NZ):
             pieces[i] = joined(512 + i * 32, 16)
 
@@ -281,16 +294,21 @@
         norms = jnp.where(low, other, part)
         return norms, jnp.where(low, part, other) / norms + NOISE_LEVEL
 
-    arrived(4, vb0)
-    train_product(kr, vb0)
-    push(7, line, lambda i: kr.at[i], krb.at[z])
+    train_product(
+        kr,
+        18,
+        vb0,
+        lambda first: push(
+            7, line[first : first + 4], lambda k: kr.at[place_of(k)], krb.at[z]
+        ),
+    )
     arrived(5, r0l)
     curve = fold(jnp.sum(kr[...] * r0l[...], axis=0))
     part = jnp.where(low, curve, rr_own)
     sa_s[...] = part
     sa[q] = part
     push(8, plane, sa_s, sa.at[q])
-    krb[z] = kr[z]
+    krb[z] = kr[place_of(0)]
     cand_product(ucs, vb0)
 
     arrived(2, xcb)
@@ -309,7 +327,7 @@
     part = jnp.sum(sa[...], axis=0)
     sb_s[...] = part
     sb[z] = part
-    push(10, line, lambda i: sb_s, sb.at[z])
+    push(10, line, sb_s, sb.at[z])
     norms, quotient = ratio(part)
     share = jnp.where(norms > 0.0, quotient, 0.0)
     arrived(7, krb)
@@ -317,12 +335,12 @@
     image = jnp.sum(krb[...], axis=0) + NOISE_LEVEL * r0
 
     own1[...] = image
-    q0l[z] = image
+    q0l[place_of(0)] = image
     high = (image - share * r0).astype(BF16)
     hb1[...] = high
-    vb1[q] = high
-    push(11, plane, hb1, vb1.at[q])
-    push(12, line, lambda i: own1, q0l.at[z])
+    vb1[sub] = high
+    gather(22, hb1, vb1)
+    push(12, line, own1, lambda k: q0l.at[place_of(-k)])
     arrived(10, sb)
     rr0, quotient = ratio(jnp.sum(sb[...], axis=0))
     alpha1 = 1.0 / quotient
@@ -331,12 +349,11 @@
     ra_s[...] = rr1_own
     ra[q] = rr1_own
     push(13, plane, ra_s, ra.at[q])
-    push(9, line, lambda i: ucs.at[i], ucb.at[z])
+    push(9, line, lambda k: ucs.at[zs[k]], ucb.at[z])
     ucb[z] = ucs[z]
-    push(6, cands, lambda i: pcs.at[i], pcb.at[c])
+    push(6, cands, lambda tag: pcs.at[xs[tag[0]] * 2 + tag[1]], pcb.at[c])
     mixed_own = fold(r0 * r1)
-    arrived(11, vb1)
-    train_product(kq, vb1)
+    train_product(kq, 22, vb1, lambda first: None)
     arrived(12, q0l)
     r1l = r0l[...] - alpha1 * q0l[...]
     k1 = (1.0 - alpha1 * share) * kr[...] - alpha1 * kq[...]
@@ -350,16 +367,16 @@
     part = jnp.sum(ra[...], axis=0)
     rb_s[...] = part
     rb[z] = part
-    push(14, line, lambda i: rb_s, rb.at[z])
+    push(14, line, rb_s, rb.at[z])
     cand_product(wcs, vb1)
     wcs[...] = wcs[...] + share * ucs[...]
-    push(15, line, lambda i: wcs.at[i], wcb.at[z])
+    push(15, line, lambda k: wcs.at[zs[k]], wcb.at[z])
     wcb[z] = wcs[z]
     arrived(16, qa)
     part = jnp.sum(qa[...], axis=0)
     qb_s[...] = part
     qb[z] = part
-    push(17, line, lambda i: qb_s, qb.at[z])
+    push(17, line, qb_s, qb.at[z])
     arrived(6, pcb)
     prior = jnp.sum(pcb[...], axis=0)
     arrived(9, ucb)
@@ -378,17 +395,25 @@
     curve, mixed = jnp.where(low, part, other), jnp.where(low, other, part)
     alpha2 = rr1 / (curve + beta * (mixed + beta * (rr0 / alpha1)))
 
-    result = alpha1 * r0 + alpha2 * d1
-    sol[0:32, :] = result[:, 0:64]
-    sol[32:64, :] = swap(result)[:, 0:64]
-    result = prior + (alpha1 + alpha2 * beta) * first_part + alpha2 * second_part
-    sam[0:16, :] = result[:, 0:64]
-    sam[16:32, :] = swap(result)[:, 0:64]
-
-    for phase, buf in enumerate(
-        (xp, xl, xcb, ptb, vb0, r0l, pcb, krb, sa, ucb, sb, vb1, q0l, ra, rb, wcb, qa, qb)
-    ):
+    packed[0:32, :] = alpha1 * r0 + alpha2 * d1
+    packed[32:48, :] = prior + (alpha1 + alpha2 * beta) * first_part + alpha2 * second_part
+
+    whole = {
+        0: xp, 1: xl, 2: xcb, 3: ptb, 5: r0l, 6: pcb, 7: krb, 8: sa, 9: ucb, 10: sb,
+        12: q0l, 13: ra, 14: rb, 15: wcb, 16: qa, 17: qb,
+    }
+    for phase, buf in whole.items():
         settle(phase, ssem, buf)
+    for base, buf in ((18, vb0), (22, vb1)):
+        for i in range(4):
+            settle(base + i, ssem, buf, 7 if i == 0 else 8)
+
+
+def unpack(packed, sam, sol):
+    sol[0:32, :] = packed[0:32, 0:64]
+    sol[32:64, :] = pltpu.roll(packed[0:32, :], 64, 1)[:, 0:64]
+    sam[0:16, :] = packed[32:48, 0:64]
+    sam[16:32, :] = pltpu.roll(packed[32:48, :], 64, 1)[:, 0:64]
 
 
 def body(x_train, x_cand, targets, noise, omega, phase, prior_weights):
@@ -410,26 +435,33 @@
         row, field(NP, 1), row, field(NZ, 1), row, field(NP, 1), row, field(NZ, 1),
         row, field(NP, 1), row, field(NZ, 1),
         vmem((32, 128), BF16), vmem((32, 128), BF16),
-        pltpu.SemaphoreType.DMA((8,)), pltpu.SemaphoreType.DMA((18,)),
-        pltpu.SemaphoreType.DMA((18,)),
+        pltpu.SemaphoreType.DMA((8,)), pltpu.SemaphoreType.DMA((26,)),
+        pltpu.SemaphoreType.DMA((26,)),
     ]
     operands = (
         x_train, x_cand, targets.reshape(1, OWN), noise, omega,
         phase.reshape(1, TOTAL_FEATS), prior_weights.T,
     )
-    return pl.pallas_call(
+    packed = pl.pallas_call(
         kernel,
-        out_shape=(
-            jax.ShapeDtypeStruct((CANDS, OWN), F32),
-            jax.ShapeDtypeStruct((OWN, OWN), F32),
-        ),
+        out_shape=jax.ShapeDtypeStruct((48, 128), F32),
         in_specs=[pl.BlockSpec(memory_space=pltpu.HBM)] * 7,
-        out_specs=(pl.BlockSpec(memory_space=vmem),) * 2,
+        out_specs=pl.BlockSpec(memory_space=vmem),
         scratch_shapes=scratch,
         compiler_params=pltpu.CompilerParams(
             collective_id=0, has_side_effects=True, vmem_limit_bytes=32 * 1024 * 1024
         ),
     )(*(pltpu.with_memory_space_constraint(value, pltpu.HBM) for value in operands))
+    return pl.pallas_call(
+        unpack,
+        out_shape=(
+            jax.ShapeDtypeStruct((CANDS, OWN), F32),
+            jax.ShapeDtypeStruct((OWN, OWN), F32),
+        ),
+        in_specs=[pl.BlockSpec(memory_space=vmem)],
+        out_specs=(pl.BlockSpec(memory_space=vmem),) * 2,
+        compiler_params=pltpu.CompilerParams(vmem_limit_bytes=4 * 1024 * 1024),
+    )(packed)
 
 
 def solution(mesh):

time: 44.4 us -> 43.9 us (0.989)
  local copies, waits for them, and re-layouts: 1.22 us -> 0 us
  Pallas kernels: 42.4 us -> 43.1 us
    unnamed x2 -> x0, local copies, waits for them, and re-layouts: 1.22 us -> none
    pallas_call x1 -> x2, Pallas kernels: 42.4 us -> 43.1 us  [the longest x1 42.5 us: body(): pl.pallas_call(kernel, out_shape=jax.ShapeDtypeStruct((48, 128), F32), in...]
where the time goes in v4:
time: 43.9 us; the launch traced here: 43.8 us
  Pallas kernels  43.1 us (98%)
  between operations  0.64 us (1%)
    pallas_call x1, Pallas kernels, body(): pl.pallas_call(kernel, out_shape=jax.ShapeDtypeStruct((48, 128), F32), in...  42.5 us

profile of v4, /device:TPU:1, one launch (start us, length us, event | category | flops | bytes accessed | tf_op | source)
XLA Modules:
  0.0 43.8 jit_solution(7522711504675118684)
XLA Ops:
  0.6 42.5 %shard_map.86.packed = f32[48,128]{1,0:T(8,128)S(1)} custom-call(f32[8,512]{1,0:T(8,128)} %xt_hbm.1, f32[8,1024]{1,0:T(8,128)} %xc_hbm.1, f32[1,64]{1,0:T(1,128)} %bitcast.5, f32[64,64]{1,0:T(8,128)} %nz_hbm.1, f32[8,4096]{1,0:T(8,128)} %om_hbm.1, f32[1,4096]{1,0:T(1,128)} %bitcast.4, bf16[64,512]{1,0:T(8,128)(2,1)} %bitcast.3), custom_call_target="tpu_custom_call" | custom-call | tf_op jit(solution)/shard_map/pallas_call | solution.py:445
  43.1 0.7 %shard_map.87 = (f32[32,64]{1,0:T(8,128)}, f32[64,64]{1,0:T(8,128)}) custom-call(f32[48,128]{1,0:T(8,128)S(1)} %shard_map.86.packed), custom_call_target="tpu_custom_call" | custom-call | tf_op jit(solution)/shard_map/pallas_call | solution.py:455

commit v5 on v4

--- a/solution.py
+++ b/solution.py
@@ -16,11 +16,19 @@
 FEATS = 512
 TOTAL_FEATS = 4096
 NOISE_LEVEL = 0.5
+def hops(offset):
+    dx, dy, dz, _ = offset
+    return min(dx, 4 - dx) + min(dy, 4 - dy) + min(dz, NZ - dz)
+
+
 PLANE_ORDER = sorted(
-    ((i, j, k) for i in range(4) for j in range(4) for k in range(2) if i + j + k),
-    key=lambda d: -(min(d[0], 4 - d[0]) + min(d[1], 4 - d[1])),
+    ((i, j, 0, k) for i in range(4) for j in range(4) for k in range(2) if i + j + k),
+    key=lambda offset: -hops(offset),
 )
 LINE_ORDER = (4, 3, 5, 2, 6, 1, 7, 0)
+GREETING = sorted(
+    [(0, 0, k, 0) for k in LINE_ORDER[:-1]] + PLANE_ORDER, key=lambda offset: -hops(offset)
+)
 
 
 def place_of(k):
@@ -73,7 +81,7 @@
     pts, ptb, pcs, pcb, own0, own1, vb0, vb1, r0l, q0l,
     o1, o2, kr, krb, kq, ucs, ucb, wcs, wcb,
     sa_s, sa, sb_s, sb, ra_s, ra, rb_s, rb, qa_s, qa, qb_s, qb,
-    hb0, hb1, isem, ssem, rsem,
+    isem, ssem, rsem,
 ):
     t, c = lax.axis_index("train"), lax.axis_index("cand")
     y_hi, z, core = t // 16, lax.rem(t, 16) // 2, lax.rem(t, 2)
@@ -94,7 +102,7 @@
             xs[dx] * 2 + lax.rem(ys[dy], 2),
         )
 
-    plane = [(device(i, j, 0, k), i) for i, j, k in PLANE_ORDER]
+    plane = [(device(*offset), offset[0]) for offset in PLANE_ORDER]
     line = [(device(0, 0, k, 0), k) for k in LINE_ORDER[:-1]]
     blocks = [(device(0, j, 0, k), None) for j, k in ((2, 1), (2, 0), (0, 1))]
     near = 1 - y_lo
@@ -123,7 +131,8 @@
     barrier = pltpu.get_barrier_semaphore()
     for copy in inputs[:5]:
         copy.start()
-    for peer, _ in plane + line:
+    for offset in GREETING:
+        peer = device(*offset)
         pl.semaphore_signal(barrier, inc=1, device_id=peer, device_id_type=MESH)
     for copy in inputs[5:]:
         copy.start()
@@ -147,8 +156,13 @@
     def arrived(phase, buf, count=None):
         settle(phase, rsem, buf, count)
 
-    def gather(base, source, target):
-        push(lambda i: base + -i % 4, plane, source, lambda i: target.at[(-i % 4) * 8 + sub])
+    def gather(base, field):
+        push(
+            lambda i: base + -i % 4,
+            plane,
+            field.at[sub],
+            lambda i: field.at[(-i % 4) * 8 + sub],
+        )
 
     lane = lax.broadcasted_iota(jnp.int32, (1, 128), 1)
     low = lane < 64
@@ -222,6 +236,20 @@
             pair(line_cands(2 * j), line_cands(2 * j + 1))
         )
 
+    def entries(first, count):
+        rows = pl.ds(first, count)
+        power = jnp.dot(atl[rows, :], by[...], preferred_element_type=F32)
+        km[rows, :] = jnp.exp(power).astype(BF16)
+
+    arrived(3, ptb)
+    r0 = base - jnp.sum(ptb[...], axis=0)
+    own0[...] = r0
+    r0l[place_of(0)] = r0
+    vb0[sub] = r0.astype(BF16)
+    gather(18, vb0)
+    push(5, line, own0, lambda k: r0l.at[place_of(-k)])
+    rr_own = fold(r0 * r0)
+
     arrived(0, xp)
     for i in range(4):
         tiles = [xp[g, :, pl.ds(pl.multiple_of(xs[i] * 128, 128), 128)] for g in range(NH)]
@@ -233,59 +261,34 @@
             tail = rows8(ones, ones, ones, *split3(half_norm(points)))
             by[:, start : start + 256] = right_side(points, tail)
 
-    def entries(first, count):
-        rows = pl.ds(first, count)
-        power = jnp.dot(atl[rows, :], by[...], preferred_element_type=F32)
-        km[rows, :] = jnp.exp(power).astype(BF16)
-
-    arrived(3, ptb)
-    r0 = base - jnp.sum(ptb[...], axis=0)
-    own0[...] = r0
-    r0l[place_of(0)] = r0
-    hb0[...] = r0.astype(BF16)
-    vb0[sub] = r0.astype(BF16)
-    gather(18, hb0, vb0)
-    push(5, line, own0, lambda k: r0l.at[place_of(-k)])
-    rr_own = fold(r0 * r0)
-
     arrived(1, xl)
     for j in range(4):
         atl[j * 128 : j * 128 + 128, :] = left_side(pair(xl[2 * j], xl[2 * j + 1]))
     entries(0, 512)
     entries(512, 256)
 
-    def group_product(first, count, field, i, fresh):
+    def multiply(first, count, field):
         rows = pl.ds(first, count)
-        values = field[8 * i : 8 * i + 8].reshape(256, 128)
-        for start, out in ((0, o1), (1024, o2)):
-            term = jnp.dot(
-                km[rows, start + 256 * i : start + 256 * i + 256],
-                values,
-                preferred_element_type=F32,
-            )
-            out[rows, :] = term if fresh else out[rows, :] + term
+        values = field[...].reshape(NP * 32, 128)
+        o1[rows, :] = jnp.dot(km[rows, 0:1024], values, preferred_element_type=F32)
+        o2[rows, :] = jnp.dot(km[rows, 1024:2048], values, preferred_element_type=F32)
 
     def joined(first, size):
         a1, b1 = o1[pl.ds(first, size), :], o1[pl.ds(first + size, size), :]
         a2, b2 = o2[pl.ds(first, size), :], o2[pl.ds(first + size, size), :]
         return jnp.where(low, a1, b2) + swap(jnp.where(low, b1, a2))
 
-    def train_product(pieces, base, field, ready):
+    def gathered(base, field):
         for i in range(4):
             arrived(base + i, field, 7 if i == 0 else 8)
-        values = field[...].reshape(NP * 32, 128)
-        for first in (0, 4):
-            rows = pl.ds(64 * first, 256)
-            o1[rows, :] = jnp.dot(km[rows, 0:1024], values, preferred_element_type=F32)
-            o2[rows, :] = jnp.dot(km[rows, 1024:2048], values, preferred_element_type=F32)
-            for k in range(first, first + 4):
-                pieces[k] = joined(64 * k, 32)
-            ready(first)
+
+    def train_product(first, count, pieces, field):
+        multiply(64 * first, 64 * count, field)
+        for k in range(first, first + count):
+            pieces[k] = joined(64 * k, 32)
 
     def cand_product(pieces, field):
-        values = field[...].reshape(NP * 32, 128)
-        o1[512:768, :] = jnp.dot(km[512:768, 0:1024], values, preferred_element_type=F32)
-        o2[512:768, :] = jnp.dot(km[512:768, 1024:2048], values, preferred_element_type=F32)
+        multiply(512, 256, field)
         for i in range(NZ):
             pieces[i] = joined(512 + i * 32, 16)
 
@@ -294,14 +297,10 @@
         norms = jnp.where(low, other, part)
         return norms, jnp.where(low, part, other) / norms + NOISE_LEVEL
 
-    train_product(
-        kr,
-        18,
-        vb0,
-        lambda first: push(
-            7, line[first : first + 4], lambda k: kr.at[place_of(k)], krb.at[z]
-        ),
-    )
+    gathered(18, vb0)
+    for first in (0, 4):
+        train_product(first, 4, kr, vb0)
+        push(7, line[first : first + 4], lambda k: kr.at[place_of(k)], krb.at[z])
     arrived(5, r0l)
     curve = fold(jnp.sum(kr[...] * r0l[...], axis=0))
     part = jnp.where(low, curve, rr_own)
@@ -336,10 +335,8 @@
 
     own1[...] = image
     q0l[place_of(0)] = image
-    high = (image - share * r0).astype(BF16)
-    hb1[...] = high
-    vb1[sub] = high
-    gather(22, hb1, vb1)
+    vb1[sub] = (image - share * r0).astype(BF16)
+    gather(22, vb1)
     push(12, line, own1, lambda k: q0l.at[place_of(-k)])
     arrived(10, sb)
     rr0, quotient = ratio(jnp.sum(sb[...], axis=0))
@@ -353,7 +350,8 @@
     ucb[z] = ucs[z]
     push(6, cands, lambda tag: pcs.at[xs[tag[0]] * 2 + tag[1]], pcb.at[c])
     mixed_own = fold(r0 * r1)
-    train_product(kq, 22, vb1, lambda first: None)
+    gathered(22, vb1)
+    train_product(0, NZ, kq, vb1)
     arrived(12, q0l)
     r1l = r0l[...] - alpha1 * q0l[...]
     k1 = (1.0 - alpha1 * share) * kr[...] - alpha1 * kq[...]
@@ -434,7 +432,6 @@
         field(NZ, 16), field(NZ, 16), field(NZ, 16), field(NZ, 16),
         row, field(NP, 1), row, field(NZ, 1), row, field(NP, 1), row, field(NZ, 1),
         row, field(NP, 1), row, field(NZ, 1),
-        vmem((32, 128), BF16), vmem((32, 128), BF16),
         pltpu.SemaphoreType.DMA((8,)), pltpu.SemaphoreType.DMA((26,)),
         pltpu.SemaphoreType.DMA((26,)),
     ]

time: 43.9 us -> 43.3 us (0.986)
  Pallas kernels: 43.1 us -> 42.5 us
    pallas_call x1, Pallas kernels: 42.5 us -> 41.8 us  [body(): pl.pallas_call(kernel, out_shape=jax.ShapeDtypeStruct((48, 128), F32), in...]
where the time goes in v5:
time: 43.3 us; the launch traced here: 43.2 us
  Pallas kernels  42.5 us (98%)
  between operations  0.64 us (1%)
    pallas_call x1, Pallas kernels, body(): pl.pallas_call(kernel, out_shape=jax.ShapeDtypeStruct((48, 128), F32), in...  41.8 us

profile of v5, /device:TPU:1, one launch (start us, length us, event | category | flops | bytes accessed | tf_op | source)
XLA Modules:
  0.0 43.2 jit_solution(14491764841086793779)
XLA Ops:
  0.6 41.8 %shard_map.86.packed = f32[48,128]{1,0:T(8,128)S(1)} custom-call(f32[8,512]{1,0:T(8,128)} %xt_hbm.1, f32[8,1024]{1,0:T(8,128)} %xc_hbm.1, f32[1,64]{1,0:T(1,128)} %bitcast.5, f32[64,64]{1,0:T(8,128)} %nz_hbm.1, f32[8,4096]{1,0:T(8,128)} %om_hbm.1, f32[1,4096]{1,0:T(1,128)} %bitcast.4, bf16[64,512]{1,0:T(8,128)(2,1)} %bitcast.3), custom_call_target="tpu_custom_call" | custom-call | tf_op jit(solution)/shard_map/pallas_call | solution.py:442
  42.5 0.7 %shard_map.87 = (f32[32,64]{1,0:T(8,128)}, f32[64,64]{1,0:T(8,128)}) custom-call(f32[48,128]{1,0:T(8,128)S(1)} %shard_map.86.packed), custom_call_target="tpu_custom_call" | custom-call | tf_op jit(solution)/shard_map/pallas_call | solution.py:452

commit v6 on v5

--- a/solution.py
+++ b/solution.py
@@ -25,6 +25,17 @@
     ((i, j, 0, k) for i in range(4) for j in range(4) for k in range(2) if i + j + k),
     key=lambda offset: -hops(offset),
 )
+EVERYONE = sorted(
+    (
+        (i, j, k, core)
+        for i in range(4)
+        for j in range(4)
+        for k in range(NZ)
+        for core in range(2)
+        if i + j + k + core
+    ),
+    key=lambda offset: -hops(offset),
+)
 LINE_ORDER = (4, 3, 5, 2, 6, 1, 7, 0)
 GREETING = sorted(
     [(0, 0, k, 0) for k in LINE_ORDER[:-1]] + PLANE_ORDER, key=lambda offset: -hops(offset)
@@ -80,7 +91,7 @@
     xls, xl, xcs, xcb, xp, by, bw, atl, km,
     pts, ptb, pcs, pcb, own0, own1, vb0, vb1, r0l, q0l,
     o1, o2, kr, krb, kq, ucs, ucb, wcs, wcb,
-    sa_s, sa, sb_s, sb, ra_s, ra, rb_s, rb, qa_s, qa, qb_s, qb,
+    sa_s, sa, sb_s, sb, ra_s, ra, rb_s, rb, qa_s, qa,
     isem, ssem, rsem,
 ):
     t, c = lax.axis_index("train"), lax.axis_index("cand")
@@ -103,6 +114,7 @@
         )
 
     plane = [(device(*offset), offset[0]) for offset in PLANE_ORDER]
+    everyone = [(device(*offset), None) for offset in EVERYONE]
     line = [(device(0, 0, k, 0), k) for k in LINE_ORDER[:-1]]
     blocks = [(device(0, j, 0, k), None) for j, k in ((2, 1), (2, 0), (0, 1))]
     near = 1 - y_lo
@@ -359,8 +371,8 @@
     mixed = fold(jnp.sum(r0l[...] * k1 + r1l * kr[...], axis=0)) + 2.0 * NOISE_LEVEL * mixed_own
     part = jnp.where(low, curve, mixed)
     qa_s[...] = part
-    qa[q] = part
-    push(16, plane, qa_s, qa.at[q])
+    qa[z * NP + q] = part
+    push(16, everyone, qa_s, qa.at[z * NP + q])
     arrived(13, ra)
     part = jnp.sum(ra[...], axis=0)
     rb_s[...] = part
@@ -370,11 +382,6 @@
     wcs[...] = wcs[...] + share * ucs[...]
     push(15, line, lambda k: wcs.at[zs[k]], wcb.at[z])
     wcb[z] = wcs[z]
-    arrived(16, qa)
-    part = jnp.sum(qa[...], axis=0)
-    qb_s[...] = part
-    qb[z] = part
-    push(17, line, qb_s, qb.at[z])
     arrived(6, pcb)
     prior = jnp.sum(pcb[...], axis=0)
     arrived(9, ucb)
@@ -387,8 +394,8 @@
     r0 = own0[...]
     r1 = r0 - alpha1 * own1[...]
     d1 = r1 + beta * r0
-    arrived(17, qb)
-    part = jnp.sum(qb[...], axis=0)
+    arrived(16, qa)
+    part = jnp.sum(qa[...], axis=0)
     other = swap(part)
     curve, mixed = jnp.where(low, part, other), jnp.where(low, other, part)
     alpha2 = rr1 / (curve + beta * (mixed + beta * (rr0 / alpha1)))
@@ -398,7 +405,7 @@
 
     whole = {
         0: xp, 1: xl, 2: xcb, 3: ptb, 5: r0l, 6: pcb, 7: krb, 8: sa, 9: ucb, 10: sb,
-        12: q0l, 13: ra, 14: rb, 15: wcb, 16: qa, 17: qb,
+        12: q0l, 13: ra, 14: rb, 15: wcb, 16: qa,
     }
     for phase, buf in whole.items():
         settle(phase, ssem, buf)
@@ -431,7 +438,7 @@
         field(NZ, 32), field(NZ, 32), field(NZ, 32),
         field(NZ, 16), field(NZ, 16), field(NZ, 16), field(NZ, 16),
         row, field(NP, 1), row, field(NZ, 1), row, field(NP, 1), row, field(NZ, 1),
-        row, field(NP, 1), row, field(NZ, 1),
+        row, field(NZ * NP, 1),
         pltpu.SemaphoreType.DMA((8,)), pltpu.SemaphoreType.DMA((26,)),
         pltpu.SemaphoreType.DMA((26,)),
     ]

time: 43.3 us -> 43.2 us (level)
  no operation moved by 1% of the time
where the time goes in v6:
time: 43.2 us; the launch traced here: 43 us
  Pallas kernels  42.4 us (98%)
  between operations  0.64 us (1%)
    pallas_call x1, Pallas kernels, body(): pl.pallas_call(kernel, out_shape=jax.ShapeDtypeStruct((48, 128), F32), in...  41.7 us

profile of v6, /device:TPU:1, one launch (start us, length us, event | category | flops | bytes accessed | tf_op | source)
XLA Modules:
  0.0 43.0 jit_solution(5840115352710338632)
XLA Ops:
  0.6 41.7 %shard_map.86.packed = f32[48,128]{1,0:T(8,128)S(1)} custom-call(f32[8,512]{1,0:T(8,128)} %xt_hbm.1, f32[8,1024]{1,0:T(8,128)} %xc_hbm.1, f32[1,64]{1,0:T(1,128)} %bitcast.5, f32[64,64]{1,0:T(8,128)} %nz_hbm.1, f32[8,4096]{1,0:T(8,128)} %om_hbm.1, f32[1,4096]{1,0:T(1,128)} %bitcast.4, bf16[64,512]{1,0:T(8,128)(2,1)} %bitcast.3), custom_call_target="tpu_custom_call" | custom-call | tf_op jit(solution)/shard_map/pallas_call | solution.py:449
  42.3 0.7 %shard_map.87 = (f32[32,64]{1,0:T(8,128)}, f32[64,64]{1,0:T(8,128)}) custom-call(f32[48,128]{1,0:T(8,128)S(1)} %shard_map.86.packed), custom_call_target="tpu_custom_call" | custom-call | tf_op jit(solution)/shard_map/pallas_call | solution.py:459

commit v7 on v6

--- a/solution.py
+++ b/solution.py
@@ -37,9 +37,6 @@
     key=lambda offset: -hops(offset),
 )
 LINE_ORDER = (4, 3, 5, 2, 6, 1, 7, 0)
-GREETING = sorted(
-    [(0, 0, k, 0) for k in LINE_ORDER[:-1]] + PLANE_ORDER, key=lambda offset: -hops(offset)
-)
 
 
 def place_of(k):
@@ -143,8 +140,8 @@
     barrier = pltpu.get_barrier_semaphore()
     for copy in inputs[:5]:
         copy.start()
-    for offset in GREETING:
-        peer = device(*offset)
+    greeted = line[:3] + cands[:2] + line[3:5] + cands[2:6] + blocks + line[5:] + cands[6:]
+    for peer, _ in greeted:
         pl.semaphore_signal(barrier, inc=1, device_id=peer, device_id_type=MESH)
     for copy in inputs[5:]:
         copy.start()
@@ -211,7 +208,7 @@
     out = prior_share(left_side(xt[...]))
     for i in range(NC):
         pts[i] = jnp.where(low, out[64 * i : 64 * i + 32], out[64 * i + 32 : 64 * i + 64])
-    pl.semaphore_wait(barrier, NP - 1 + NZ - 1)
+    pl.semaphore_wait(barrier, len(greeted))
     push(3, cands, lambda tag: pts.at[xs[tag[0]] * 2 + tag[1]], ptb.at[c])
     for copy in inputs[5:]:
         copy.wait()
@@ -373,15 +370,15 @@
     qa_s[...] = part
     qa[z * NP + q] = part
     push(16, everyone, qa_s, qa.at[z * NP + q])
+    cand_product(wcs, vb1)
+    wcs[...] = wcs[...] + share * ucs[...]
+    push(15, line, lambda k: wcs.at[zs[k]], wcb.at[z])
+    wcb[z] = wcs[z]
     arrived(13, ra)
     part = jnp.sum(ra[...], axis=0)
     rb_s[...] = part
     rb[z] = part
     push(14, line, rb_s, rb.at[z])
-    cand_product(wcs, vb1)
-    wcs[...] = wcs[...] + share * ucs[...]
-    push(15, line, lambda k: wcs.at[zs[k]], wcb.at[z])
-    wcb[z] = wcs[z]
     arrived(6, pcb)
     prior = jnp.sum(pcb[...], axis=0)
     arrived(9, ucb)

time: 43.2 us -> 42.4 us (0.981)
  Pallas kernels: 42.4 us -> 41.6 us
    pallas_call x1, Pallas kernels: 41.7 us -> 40.9 us  [body(): pl.pallas_call(kernel, out_shape=jax.ShapeDtypeStruct((48, 128), F32), in...]
where the time goes in v7:
time: 42.4 us; the launch traced here: 42.2 us
  Pallas kernels  41.6 us (98%)
  between operations  0.64 us (2%)
    pallas_call x1, Pallas kernels, body(): pl.pallas_call(kernel, out_shape=jax.ShapeDtypeStruct((48, 128), F32), in...  40.9 us

profile of v7, /device:TPU:1, one launch (start us, length us, event | category | flops | bytes accessed | tf_op | source)
XLA Modules:
  0.0 42.2 jit_solution(4930396691101899591)
XLA Ops:
  0.6 40.9 %shard_map.86.packed = f32[48,128]{1,0:T(8,128)S(1)} custom-call(f32[8,512]{1,0:T(8,128)} %xt_hbm.1, f32[8,1024]{1,0:T(8,128)} %xc_hbm.1, f32[1,64]{1,0:T(1,128)} %bitcast.5, f32[64,64]{1,0:T(8,128)} %nz_hbm.1, f32[8,4096]{1,0:T(8,128)} %om_hbm.1, f32[1,4096]{1,0:T(1,128)} %bitcast.4, bf16[64,512]{1,0:T(8,128)(2,1)} %bitcast.3), custom_call_target="tpu_custom_call" | custom-call | tf_op jit(solution)/shard_map/pallas_call | solution.py:446
  41.6 0.7 %shard_map.87 = (f32[32,64]{1,0:T(8,128)}, f32[64,64]{1,0:T(8,128)}) custom-call(f32[48,128]{1,0:T(8,128)S(1)} %shard_map.86.packed), custom_call_target="tpu_custom_call" | custom-call | tf_op jit(solution)/shard_map/pallas_call | solution.py:456

commit v8 on v7

--- a/solution.py
+++ b/solution.py
@@ -117,7 +117,9 @@
     near = 1 - y_lo
     cands = [
         ((t, xs[i] * 2 + j), (i, j))
-        for i, j in ((2, 0), (2, 1), (1, 0), (1, 1), (3, 0), (3, 1), (0, near))
+        for i, j in (
+            (2, near), (1, near), (3, near), (2, y_lo), (1, y_lo), (3, y_lo), (0, near),
+        )
     ]
     sub = h * 2 + y_lo
 

time: 42.4 us -> 42.4 us (level)
  no operation moved by 1% of the time
where the time goes in v8:
time: 42.4 us; the launch traced here: 42.2 us
  Pallas kernels  41.6 us (98%)
  between operations  0.64 us (2%)
    pallas_call x1, Pallas kernels, body(): pl.pallas_call(kernel, out_shape=jax.ShapeDtypeStruct((48, 128), F32), in...  40.9 us

profile of v8, /device:TPU:1, one launch (start us, length us, event | category | flops | bytes accessed | tf_op | source)
XLA Modules:
  0.0 42.2 jit_solution(6249378721915812192)
XLA Ops:
  0.6 40.9 %shard_map.86.packed = f32[48,128]{1,0:T(8,128)S(1)} custom-call(f32[8,512]{1,0:T(8,128)} %xt_hbm.1, f32[8,1024]{1,0:T(8,128)} %xc_hbm.1, f32[1,64]{1,0:T(1,128)} %bitcast.5, f32[64,64]{1,0:T(8,128)} %nz_hbm.1, f32[8,4096]{1,0:T(8,128)} %om_hbm.1, f32[1,4096]{1,0:T(1,128)} %bitcast.4, bf16[64,512]{1,0:T(8,128)(2,1)} %bitcast.3), custom_call_target="tpu_custom_call" | custom-call | tf_op jit(solution)/shard_map/pallas_call | solution.py:448
  41.5 0.7 %shard_map.87 = (f32[32,64]{1,0:T(8,128)}, f32[64,64]{1,0:T(8,128)}) custom-call(f32[48,128]{1,0:T(8,128)S(1)} %shard_map.86.packed), custom_call_target="tpu_custom_call" | custom-call | tf_op jit(solution)/shard_map/pallas_call | solution.py:458

commit v9 on v8

--- a/solution.py
+++ b/solution.py
@@ -393,14 +393,10 @@
     r0 = own0[...]
     r1 = r0 - alpha1 * own1[...]
     d1 = r1 + beta * r0
-    arrived(16, qa)
-    part = jnp.sum(qa[...], axis=0)
-    other = swap(part)
-    curve, mixed = jnp.where(low, part, other), jnp.where(low, other, part)
-    alpha2 = rr1 / (curve + beta * (mixed + beta * (rr0 / alpha1)))
-
-    packed[0:32, :] = alpha1 * r0 + alpha2 * d1
-    packed[32:48, :] = prior + (alpha1 + alpha2 * beta) * first_part + alpha2 * second_part
+    first_step = alpha1 * r0
+    first_sample = prior + alpha1 * first_part
+    sample_step = beta * first_part + second_part
+    first_square = beta * beta * (rr0 / alpha1)
 
     whole = {
         0: xp, 1: xl, 2: xcb, 3: ptb, 5: r0l, 6: pcb, 7: krb, 8: sa, 9: ucb, 10: sb,
@@ -411,6 +407,14 @@
     for base, buf in ((18, vb0), (22, vb1)):
         for i in range(4):
             settle(base + i, ssem, buf, 7 if i == 0 else 8)
+
+    arrived(16, qa)
+    part = jnp.sum(qa[...], axis=0)
+    other = swap(part)
+    curve, mixed = jnp.where(low, part, other), jnp.where(low, other, part)
+    alpha2 = rr1 / (curve + beta * mixed + first_square)
+    packed[0:32, :] = first_step + alpha2 * d1
+    packed[32:48, :] = first_sample + alpha2 * sample_step
 
 
 def unpack(packed, sam, sol):

time: 42.4 us -> 42.4 us (level)
  no operation moved by 1% of the time
where the time goes in v9:
time: 42.4 us; the launch traced here: 42.2 us
  Pallas kernels  41.6 us (98%)
  between operations  0.64 us (2%)
    pallas_call x1, Pallas kernels, body(): pl.pallas_call(kernel, out_shape=jax.ShapeDtypeStruct((48, 128), F32), in...  40.9 us

profile of v9, /device:TPU:1, one launch (start us, length us, event | category | flops | bytes accessed | tf_op | source)
XLA Modules:
  0.0 42.2 jit_solution(5464078146174255535)
XLA Ops:
  0.6 40.9 %shard_map.86.packed = f32[48,128]{1,0:T(8,128)S(1)} custom-call(f32[8,512]{1,0:T(8,128)} %xt_hbm.1, f32[8,1024]{1,0:T(8,128)} %xc_hbm.1, f32[1,64]{1,0:T(1,128)} %bitcast.5, f32[64,64]{1,0:T(8,128)} %nz_hbm.1, f32[8,4096]{1,0:T(8,128)} %om_hbm.1, f32[1,4096]{1,0:T(1,128)} %bitcast.4, bf16[64,512]{1,0:T(8,128)(2,1)} %bitcast.3), custom_call_target="tpu_custom_call" | custom-call | tf_op jit(solution)/shard_map/pallas_call | solution.py:452
  41.5 0.7 %shard_map.87 = (f32[32,64]{1,0:T(8,128)}, f32[64,64]{1,0:T(8,128)}) custom-call(f32[48,128]{1,0:T(8,128)S(1)} %shard_map.86.packed), custom_call_target="tpu_custom_call" | custom-call | tf_op jit(solution)/shard_map/pallas_call | solution.py:462

commit v10 on v9

--- a/solution.py
+++ b/solution.py
@@ -140,12 +140,10 @@
         )
     ]
     barrier = pltpu.get_barrier_semaphore()
-    for copy in inputs[:5]:
-        copy.start()
     greeted = line[:3] + cands[:2] + line[3:5] + cands[2:6] + blocks + line[5:] + cands[6:]
     for peer, _ in greeted:
         pl.semaphore_signal(barrier, inc=1, device_id=peer, device_id_type=MESH)
-    for copy in inputs[5:]:
+    for copy in inputs:
         copy.start()
 
     def push(phase, peers, source, target):

time: 42.4 us -> 42.4 us (level)
  no operation moved by 1% of the time
where the time goes in v10:
time: 42.4 us; the launch traced here: 42.2 us
  Pallas kernels  41.6 us (98%)
  between operations  0.64 us (2%)
    pallas_call x1, Pallas kernels, body(): pl.pallas_call(kernel, out_shape=jax.ShapeDtypeStruct((48, 128), F32), in...  40.9 us

profile of v10, /device:TPU:1, one launch (start us, length us, event | category | flops | bytes accessed | tf_op | source)
XLA Modules:
  0.0 42.2 jit_solution(7480267206617863942)
XLA Ops:
  0.6 40.9 %shard_map.86.packed = f32[48,128]{1,0:T(8,128)S(1)} custom-call(f32[8,512]{1,0:T(8,128)} %xt_hbm.1, f32[8,1024]{1,0:T(8,128)} %xc_hbm.1, f32[1,64]{1,0:T(1,128)} %bitcast.5, f32[64,64]{1,0:T(8,128)} %nz_hbm.1, f32[8,4096]{1,0:T(8,128)} %om_hbm.1, f32[1,4096]{1,0:T(1,128)} %bitcast.4, bf16[64,512]{1,0:T(8,128)(2,1)} %bitcast.3), custom_call_target="tpu_custom_call" | custom-call | tf_op jit(solution)/shard_map/pallas_call | solution.py:450
  41.6 0.7 %shard_map.87 = (f32[32,64]{1,0:T(8,128)}, f32[64,64]{1,0:T(8,128)}) custom-call(f32[48,128]{1,0:T(8,128)S(1)} %shard_map.86.packed), custom_call_target="tpu_custom_call" | custom-call | tf_op jit(solution)/shard_map/pallas_call | solution.py:460
